TPU v7x, 512 devices: a whole 4x8x8 slice. The times are simulated.
512 devices in a mesh: grp: 2 (over core), reg: 16 (over z, x_hi), tgt: 16 (over y, x_lo).
Axes of the slice: x: 4 (x_hi: 2, x_lo: 2; x = x_hi * 2 + x_lo), y: 8, z: 8, core: 2. Of those that a mesh axis runs over, the one named last changes fastest.
Arguments:
- expr_stretch: bfloat16 [6144, 4096], P('reg'), may hold values from -6 to 6
- target_stretch: bfloat16 [6144, 1024], P('reg', 'tgt'), may hold values from -6 to 6
- subsample: int32 [2, 6144], replicated, may hold values 0 or 1
- gram_state: float32 [2, 2, 4096, 4096], P(None, 'grp', 'reg', 'tgt')
- cross_state: float32 [2, 2, 4096, 1024], P(None, 'grp', 'reg', 'tgt'), may hold values from -10 to 10
- step_size: float32 [2], replicated, may hold values from 0.15 to 0.25
- penalty: float32 [2], replicated, may hold values from 0.3 to 1
Outputs:
- gram_sums: float32 [2, 4096, 4096], P('grp', 'reg', 'tgt')
- cross_sums: float32 [2, 4096, 1024], P('grp', 'reg', 'tgt')
- coefficients: float32 [2, 4096, 1024], P('grp', 'reg', 'tgt')
All inputs are finite; a program needn't handle non-finite values.
Results may differ from a plain program's by a relative error of at most 0.0021.
Values may be sent and summed in bfloat16 or wider, within the bound.
A program may use at most 64 MiB of HBM per device.

v0:
```python
import jax
import jax.numpy as jnp
from jax import lax
from jax.sharding import PartitionSpec as P

ITERS = 3


def partner(value, axis, distance):
    mask = 2**distance
    pairs = [(source, source ^ mask) for source in range(lax.axis_size(axis))]
    return lax.ppermute(value, axis, pairs)


def from_behind(block, axis, distance):
    devices = range(lax.axis_size(axis))
    route = [(i - distance, i) for i in devices if i - distance in devices]
    return lax.ppermute(block, axis, route)


def soften(values, threshold):
    return values - jnp.clip(values, -threshold, threshold)


def make_adder(region_cols, weight_rows, gate, running, pieces):

    def make_accumulate(carried):
        weighted = jnp.concatenate(
            [region_cols * weight_rows[which][:, None] for which in range(weight_rows.shape[0])],
            axis=1,
        )
        paired = jnp.concatenate([pieces[0], pieces[1]], axis=1)
        return lax.dot_general(
            weighted, paired, (((0,), (0,)), ((), ())), preferred_element_type=jnp.float32
        )

    return lax.cond(gate, make_accumulate, lambda carried: carried, running)


def fit_lasso(current, tgt_cols, step_vals, penalty_vals, gate):
    gram_low = current[:, :, :tgt_cols].astype(jnp.bfloat16)
    cross_now = current[:, :, tgt_cols:]
    step_scale = step_vals[:, None, None]
    threshold = step_scale * penalty_vals[:, None, None]
    beta = soften(step_scale * cross_now, threshold)
    zero_product = jnp.zeros(cross_now.shape, jnp.float32)
    gram_whole = lax.all_gather(gram_low, "tgt", axis=2, tiled=True)
    for iteration in range(ITERS - 1):
        beta_low = beta.astype(jnp.bfloat16)
        shard_piece = lax.all_gather(beta_low, "reg", axis=1, tiled=True)

        def add_accumulate(carried):
            return jnp.einsum(
                "rak,rkb->rab", gram_whole, shard_piece, preferred_element_type=jnp.float32
            )

        product = lax.cond(gate, add_accumulate, lambda carried: carried, zero_product)
        beta = soften(beta - step_scale * (product - cross_now), threshold)
    return beta


def body(expr_stretch, target_stretch, subsample, gram_state, cross_state, step_size, penalty):
    section_index = lax.axis_index("grp")
    is_gram = section_index == 0
    is_fit = section_index == 1
    reg_rows = gram_state.shape[2]
    tgt_cols = gram_state.shape[3]
    cells_all = subsample.shape[1]
    col_start = lax.axis_index("tgt") * tgt_cols
    own_cols = lax.dynamic_slice_in_dim(expr_stretch, col_start, tgt_cols, 1)
    weights_low = subsample.astype(jnp.bfloat16)
    own_current = jnp.concatenate([gram_state[0, 0], cross_state[0, 0]], axis=1)
    own_sums = jnp.concatenate([gram_state[1, 0], cross_state[1, 0]], axis=1)
    span_cols = own_sums.shape[1]
    outgoing = jnp.concatenate(
        [
            lax.dynamic_index_in_dim(gram_state[:, 0], section_index, 0, False),
            lax.dynamic_index_in_dim(cross_state[:, 0], section_index, 0, False),
        ],
        axis=1,
    )
    incoming = partner(outgoing, "grp", 0)
    region_cols = lax.all_to_all(expr_stretch, "reg", split_axis=1, concat_axis=0, tiled=True)
    start_sum = jnp.zeros((2 * reg_rows, span_cols), jnp.float32)
    stretch_term = (
        make_adder(
            region_cols,
            weights_low,
            is_gram,
            start_sum,
            (
                lax.all_gather(own_cols, "reg", axis=0, tiled=True),
                lax.all_gather(target_stretch, "reg", axis=0, tiled=True),
            ),
        )
        / cells_all
    )
    first_term = stretch_term[:reg_rows]
    second_term = stretch_term[reg_rows:]
    handed = incoming + second_term
    arrived = from_behind(handed, "grp", 1)
    summed = jnp.where(is_gram, own_sums + first_term, arrived)
    beta = fit_lasso(jnp.stack([incoming, own_current]), tgt_cols, step_size, penalty, is_fit)
    coef_back = from_behind(beta[0], "grp", -1)
    coef_out = jnp.where(is_gram, coef_back, beta[1])[None]
    gram_out = summed[None, :, :tgt_cols]
    cross_out = summed[None, :, tgt_cols:]
    return (gram_out, cross_out, coef_out)


def solution(mesh):
    return jax.shard_map(
        body,
        mesh=mesh,
        in_specs=(
            P("reg", None),
            P("reg", "tgt"),
            P(),
            P(None, "grp", "reg", "tgt"),
            P(None, "grp", "reg", "tgt"),
            P(),
            P(),
        ),
        out_specs=(P("grp", "reg", "tgt"), P("grp", "reg", "tgt"), P("grp", "reg", "tgt")),
        check_vma=False,
    )
```

profile of v0, /device:TPU:1, one launch (start us, length us, event | category | flops | bytes accessed | tf_op | source)
XLA Modules:
  0.0 439.7 jit_solution(3370947880202756983)
XLA Ops:
  7.2 0.0 copy-start.5
  7.2 0.0 copy-start.6
  7.2 0.0 all-gather.9.cloned.1.call-start
  7.2 0.0 copy-start
  7.2 1.7 slice_bitcast_fusion.3
  8.9 2.0 fusion.17
  10.9 1.1 copy.33
  12.0 0.7 pad_maximum_fusion.1
  12.8 8.8 %collective-permute-start = (f32[256,320]{0,1:T(8,128)}, f32[256,320]{0,1:T(8,128)}, u32[]{:S(2)}, u32[]{:S(2)}) collective-permute-start(f32[256,320]{0,1:T(8,128)} %pad_maximum_fusion.1), channel_id=1, source_target_pairs={{0,256},{256,0},{1,257},{257,1},{2,258},{258,2},{3,259},{259,3},{4... | collective-permute-start | bytes 983048 | tf_op jit(solution)/shard_map/ppermute | solution.py:12
  21.6 1.8 copy.41
  23.3 1.0 maximum_bitcast_fusion
  24.3 0.0 copy-done.5
  24.3 0.0 copy-done.6
  24.3 0.0 collective-permute-done
  24.4 1.6 fusion.11
  25.9 0.0 all-gather.9.cloned.1.call-update
  25.9 0.0 all-gather.7.cloned.1.call-start
  26.0 1.7 fusion.8
  27.7 0.0 all-gather.7.cloned.1.call-update
  27.7 0.0 all-gather.5.cloned.1.call-start
  27.8 0.0 copy-done
  27.8 0.7 constant_dynamic-slice_fusion.1
  28.5 0.0 all-gather.5.cloned.1.call-update
  28.5 2.9 copy.30
  31.4 7.2 %all-to-all-start = ((bf16[384,16,256]{0,2,1:T(8,128)(2,1)}), bf16[384,16,256]{0,2,1:T(8,128)(2,1)S(1)}, u32[]{:S(2)}, u32[]{:S(2)}) async-start(bf16[384,16,256]{0,2,1:T(8,128)(2,1)} %bitcast.35), calls=%async_computation | async-start | bytes 6291456 | tf_op jit(solution)/shard_map/all_to_all | solution.py:83
  38.6 0.0 all-gather.11.cloned.1.call-start
  38.7 95.5 %all-gather.9.cloned.1.call-done = bf16[2,4096,64]{1,2,0:T(8,128)(2,1)} async-done(((bf16[2,256,64]{1,2,0:T(8,128)(2,1)}), bf16[2,4096,64]{1,2,0:T(8,128)(2,1)}) %all-gather.9.cloned.1.call-update) | async-done | bytes 1048592 | tf_op jit(solution)/shard_map/all_gather | solution.py:50
  134.2 104.5 %all-gather.7.cloned.1.call-done = bf16[2,256,4096]{1,2,0:T(8,128)(2,1)} async-done(((bf16[2,256,256]{1,2,0:T(8,128)(2,1)}), bf16[2,256,4096]{1,2,0:T(8,128)(2,1)}) %all-gather.7.cloned.1.call-update) | async-done | bytes 4194320 | tf_op jit(solution)/shard_map/all_gather | solution.py:47
  238.7 0.0 copy-start.2
  238.7 0.0 copy-start.4
  238.7 3.3 conditional.4
  238.7 3.3 fusion.18
  242.1 0.0 copy-done.2
  242.1 0.7 fusion.14
  242.8 0.0 all-gather.11.cloned.1.call-update
  242.9 0.0 copy-done.4
  242.9 0.9 copy.31
  243.8 54.5 %all_gather.16 = bf16[6144,64]{1,0:T(8,128)(2,1)} all-gather(bf16[384,64]{1,0:T(8,128)(2,1)S(1)} %copy.31), channel_id=1, replica_groups=mesh['grp'=2,'reg'=16,'tgt'=16] {'reg'}, dimensions={0}, use_global_device_ids=true | all-gather | bytes 835584 | tf_op jit(solution)/shard_map/all_gather | solution.py:93
  298.4 45.4 %all-gather.5.cloned.1.call-done = bf16[6144,256]{1,0:T(8,128)(2,1)} async-done(((bf16[384,256]{1,0:T(8,128)(2,1)}), bf16[6144,256]{1,0:T(8,128)(2,1)}) %all-gather.5.cloned.1.call-update) | async-done | bytes 3145744 | tf_op jit(solution)/shard_map/all_gather | solution.py:92
  343.8 0.0 all-to-all-done
  343.8 0.0 copy-start.3
  343.8 0.1 conditional.3
  343.8 0.1 broadcast_in_dim.6
  343.9 0.1 broadcast_multiply_fusion
  343.9 1.0 slice_add_fusion
  345.0 1.3 collective-permute-start.1
  346.3 1.1 copy.40
  347.4 14.4 %collective-permute-done.1 = f32[256,320]{0,1:T(8,128)S(1)} collective-permute-done((f32[256,320]{0,1:T(8,128)S(1)}, f32[256,320]{0,1:T(8,128)S(1)}, u32[]{:S(2)}, u32[]{:S(2)}) %collective-permute-start.1) | collective-permute-done | bytes 327712 | tf_op jit(solution)/shard_map/ppermute | solution.py:18
  361.8 0.0 copy-done.3
  361.8 0.1 fusion.9
  361.9 63.3 %all-gather.11.cloned.1.call-done = bf16[2,4096,64]{1,2,0:T(8,128)(2,1)} async-done(((bf16[2,256,64]{1,2,0:T(8,128)(2,1)}), bf16[2,4096,64]{1,2,0:T(8,128)(2,1)}) %all-gather.11.cloned.1.call-update) | async-done | bytes 1048592 | tf_op jit(solution)/shard_map/all_gather | solution.py:50
  425.1 3.3 conditional.5
  425.1 3.3 fusion.19
  428.4 0.1 minimum_subtract_fusion
  428.6 2.5 collective-permute-start.2
  431.1 0.6 slice_bitcast_fusion.2
  431.7 0.8 copy.34
  432.6 0.0 collective-permute-done.2
  432.6 0.6 fusion.13
  (4 shorter events, 0.0 us)
Async XLA Ops:
  7.2 17.2 %copy-start.5 = (f32[2]{0:T(128)S(1)}, f32[2]{0:T(128)}, u32[]{:S(2)}) copy-start(f32[2]{0:T(128)} %param.18) | copy-start | bytes 28
  7.2 17.2 %copy-start.6 = (f32[2]{0:T(128)S(1)}, f32[2]{0:T(128)}, u32[]{:S(2)}) copy-start(f32[2]{0:T(128)} %param.19) | copy-start | bytes 28
  7.2 127.0 %all-gather.9.cloned.1.call-start = ((), (), s32[]{:S(2)}) async-start(), calls=%async_computation.3 | async-start | bytes 1114112 | tf_op jit(solution)/shard_map/all_gather | solution.py:50
  7.2 20.5 %copy-start = (bf16[384,4096]{1,0:T(8,128)(2,1)S(1)}, bf16[384,4096]{1,0:T(8,128)(2,1)}, u32[]{:S(2)}) copy-start(bf16[384,4096]{1,0:T(8,128)(2,1)} %param.13) | copy-start | bytes 9437188
  12.8 11.6 %collective-permute-start = (f32[256,320]{0,1:T(8,128)}, f32[256,320]{0,1:T(8,128)}, u32[]{:S(2)}, u32[]{:S(2)}) collective-permute-start(f32[256,320]{0,1:T(8,128)} %pad_maximum_fusion.1), channel_id=1, source_target_pairs={{0,256},{256,0},{1,257},{257,1},{2,258},{258,2},{3,259},{259,3},{4... | collective-permute-start | bytes 983048 | tf_op jit(solution)/shard_map/ppermute | solution.py:12
  25.9 212.8 %all-gather.7.cloned.1.call-start = ((), (), s32[]{:S(2)}) async-start(), calls=%async_computation.2 | async-start | bytes 4456448 | tf_op jit(solution)/shard_map/all_gather | solution.py:47
  27.7 316.1 %all-gather.5.cloned.1.call-start = ((), (), s32[]{:S(2)}) async-start(), calls=%async_computation.1 | async-start | bytes 3342336 | tf_op jit(solution)/shard_map/all_gather | solution.py:92
  31.4 312.4 %all-to-all-start = ((bf16[384,16,256]{0,2,1:T(8,128)(2,1)}), bf16[384,16,256]{0,2,1:T(8,128)(2,1)S(1)}, u32[]{:S(2)}, u32[]{:S(2)}) async-start(bf16[384,16,256]{0,2,1:T(8,128)(2,1)} %bitcast.35), calls=%async_computation | async-start | bytes 6291456 | tf_op jit(solution)/shard_map/all_to_all | solution.py:83
  38.6 386.5 %all-gather.11.cloned.1.call-start = ((), (), s32[]{:S(2)}) async-start(), calls=%async_computation.4 | async-start | bytes 1114112 | tf_op jit(solution)/shard_map/all_gather | solution.py:50
  238.7 3.3 copy-start.2
  238.7 4.1 copy-start.4
  343.8 18.0 %copy-start.3 = (f32[256,64]{0,1:T(8,128)S(1)}, f32[256,64]{0,1:T(8,128)}, u32[]{:S(2)}) copy-start(f32[256,64]{0,1:T(8,128)} %get-tuple-element.72) | copy-start | bytes 196612
  345.0 16.8 %collective-permute-start.1 = (f32[256,320]{0,1:T(8,128)S(1)}, f32[256,320]{0,1:T(8,128)S(1)}, u32[]{:S(2)}, u32[]{:S(2)}) collective-permute-start(f32[256,320]{0,1:T(8,128)S(1)} %slice_add_fusion), channel_id=1, source_target_pairs={{0,256},{1,257},{2,258},{3,259},{4,260},{5,261},{6,262},{7,263},{8... | collective-permute-start | bytes 983048 | tf_op jit(solution)/shard_map/ppermute | solution.py:18
  428.6 4.0 collective-permute-start.2
Sparse Core Ops, SparseCore 0:
  26.1 108.0 all-gather.8
  136.8 101.8 all-gather.6
  241.9 101.8 all-gather.4
  347.3 77.7 all-gather.10
where the time goes:
time: 440 us
  waiting for transfers between devices  323 us (73%)
  blocking collectives  54.5 us (12%)
  starting transfers between devices  19.9 us (5%)
  between operations  14 us (3%)
  local copies, waits for them, and re-layouts  13.7 us (3%)
  other arithmetic  7.68 us (2%)
  matrix products  6.63 us (2%)
    all_gather x2, waiting for transfers between devices, fit_lasso(): shard_piece = lax.all_gather(beta_low, 'reg', axis=1, tiled=True)  159 us
    all_gather x1, waiting for transfers between devices, fit_lasso(): gram_whole = lax.all_gather(gram_low, 'tgt', axis=2, tiled=True)  105 us
    all_gather x1, blocking collectives, body(): lax.all_gather(target_stretch, 'reg', axis=0, tiled=True)  54.5 us
    all_gather x1, waiting for transfers between devices, body(): lax.all_gather(own_cols, 'reg', axis=0, tiled=True)  45.4 us
    ppermute x2, waiting for transfers between devices, from_behind(): return lax.ppermute(block, axis, route)  14.4 us
  transfers between devices with their start and end apart: 8, of which 5 were waited for; matrix products, arithmetic and copies ran while one was open for 4% of the time, Pallas kernels for 0%

commit v1 on v0

v1 whole, which is shorter than its diff:
```python
import jax
import jax.numpy as jnp
from jax import lax
from jax.experimental import pallas as pl
from jax.experimental.pallas import tpu as pltpu
from jax.sharding import PartitionSpec as P

RING = 8
CELLS = 6144
F32, BF16 = jnp.float32, jnp.bfloat16
ROWS_T = (((1,), (1,)), ((), ()))


def soften(values, threshold):
    return values - jnp.clip(values, -threshold, threshold)


def kernel(
    expr, target_hbm, subsample_hbm, gram_hbm, cross_hbm, step_hbm, penalty_hbm,
    gram_out, cross_out, coef_out,
    target, subsample, gram_state, cross_state, step_size, penalty,
    gbuf, bbuf, cross_fit, bsend, acc, precv,
    cbuf, rbuf, lhs, tpad, tsend, trecv, tgt_t, wbuf, gsend,
    xsend, xpass, own_block, xrecv, end_part, end_beta, beta_keep,
    ring_send, ring_recv, spread_send, spread_recv, piece_send, piece_recv,
    part_send, part_recv, far_send, far_recv, near_send, near_recv,
    feed_send, feed_recv, end_send, end_recv, own_send, own_recv,
    swap_send, swap_recv, local_sem, load_sem,
):
    c = lax.axis_index("grp")
    reg = lax.axis_index("reg")
    tgt = lax.axis_index("tgt")
    z, xh = reg // 2, reg % 2
    y, xl = tgt // 2, tgt % 2
    x = xh * 2 + xl

    def device(core, zz=z, hi=xh, yy=y, lo=xl):
        return (core, zz * 2 + hi, yy * 2 + lo)

    def chip_x(index, core):
        return device(core, hi=index // 2, lo=index % 2)

    def remote(src, dst, send, recv, to):
        return pltpu.make_async_remote_copy(
            src_ref=src, dst_ref=dst, send_sem=send, recv_sem=recv,
            device_id=to, device_id_type=pl.DeviceIdType.MESH,
        )

    right, left = (x + 1) % 4, (x + 3) % 4
    barrier = pltpu.get_barrier_semaphore()

    def greet(peers):
        for peer in peers:
            pl.semaphore_signal(barrier, inc=1, device_id=peer, device_id_type=pl.DeviceIdType.MESH)

    def load(index, source, here):
        copy = pltpu.make_async_copy(source, here, load_sem.at[index])
        copy.start()
        return copy

    def rings(core, view_of, along_y, sent):
        def ring_copy(ring, part, way, hop, chunk):
            here = y if ring in along_y else z
            there = (here + (1 if way == 0 else RING - 1)) % RING
            view = view_of(ring, part, chunk)
            slot = ring * 2 + part
            return remote(view, view, ring_send.at[slot, way, hop - 1], ring_recv.at[slot, way, hop - 1],
                          device(core, yy=there) if ring in along_y else device(core, zz=there))

        def ring_start(ring, part):
            here = y if ring in along_y else z
            for way in range(2):
                copy = ring_copy(ring, part, way, 1, here)
                copy.start()
                sent.append(copy)

        def ring_step(ring, part, hop):
            here = y if ring in along_y else z
            for way in range(2):
                if hop == 4 and way != part:
                    continue
                chunk = (here + (RING - hop if way == 0 else hop)) % RING
                ring_copy(ring, part, way, hop, chunk).wait_recv()
                if hop < 3 or (hop == 3 and way == part):
                    copy = ring_copy(ring, part, way, hop + 1, chunk)
                    copy.start()
                    sent.append(copy)

        return ring_start, ring_step

    @pl.when(c == 1)
    def _():
        GRAM, BETA = 0, 1
        loads = [
            load(0, step_hbm, step_size), load(1, penalty_hbm, penalty),
            load(2, cross_hbm, cross_state), load(3, gram_hbm, gram_state),
        ]
        peers = [device(1, zz=(z + d) % RING) for d in (1, 7)]
        peers += [device(1, yy=(y + d) % RING) for d in (1, 7)]
        peers += [chip_x((x + d) % 4, 1) for d in (1, 2, 3)]
        peers += [chip_x(right, 0), chip_x(left, 0), device(0)]
        greet(peers)
        sent = []

        def start(copy):
            copy.start()
            sent.append(copy)

        def view_of(ring, part, chunk):
            if ring == GRAM:
                return gbuf.at[part, chunk]
            return bbuf.at[ring - BETA, part, chunk]

        ring_start, ring_step = rings(1, view_of, (GRAM,), sent)
        own_k = xl == xh

        def own_half(ref_index):
            return pl.ds(pl.multiple_of(ref_index * 64, 64), 64)

        def piece_slot(it, r, lo):
            return bbuf.at[it, r, z, own_half(lo)]

        def piece_near(it, r):
            return remote(bsend.at[it, r], piece_slot(it, r, xl), piece_send.at[it, r, 1],
                          piece_recv.at[it, r, xl], device(1, lo=1 - xl))

        def pieces_start(it, r):
            start(remote(bsend.at[it, r], piece_slot(it, r, xl), piece_send.at[it, r, 0],
                         piece_recv.at[it, r, xl], device(1, hi=1 - xh, lo=xh)))

            @pl.when(own_k)
            def _():
                pltpu.make_async_copy(
                    bsend.at[it, r], piece_slot(it, r, xl), piece_recv.at[it, r, xl]).start()

            @pl.when(jnp.logical_not(own_k))
            def _():
                piece_near(it, r).start()

        def pieces_wait(it, r):
            for lo in range(2):
                pltpu.make_async_copy(
                    bsend.at[it, r], piece_slot(it, r, lo), piece_recv.at[it, r, lo]).wait()

        def add_products(it, r, distances, first=False):
            total = None
            for distance in distances:
                k = (y + distance) % RING if it == 0 else (z + distance) % RING
                term = lax.dot_general(bbuf[it, r, k], gbuf[r, k], ROWS_T, preferred_element_type=F32)
                total = term if total is None else total + term
            acc[it, r] = total if first else acc[it, r] + total

        def part_copy(it, r):
            return remote(acc.at[it, r, own_half(1 - xl)], precv.at[it, r],
                          part_send.at[it, r], part_recv.at[it, r], device(1, lo=1 - xl))

        def step_of(r):
            return step_size[r], step_size[r] * penalty[r]

        def next_beta(it, r, beta):
            step, threshold = step_of(r)
            part_copy(it, r).wait_recv()
            product = acc[it, r, own_half(xl)] + precv[it, r]
            return soften(beta - step * (product - cross_fit[r]), threshold)

        for copy in loads:
            copy.wait()
        gbuf[1, y] = gram_state[0].astype(BF16)
        cross_fit[1] = cross_state[0]
        step, threshold = step_of(1)
        beta_one = soften(step * cross_state[0], threshold)
        bsend[0, 1] = beta_one.astype(BF16)
        pl.semaphore_wait(barrier, len(peers))

        ring_start(GRAM, 1)
        pieces_start(0, 1)
        cross_feed = remote(cross_state.at[0], cross_fit.at[0], feed_send.at[1], feed_recv.at[1], device(0))
        gram_feed = remote(gsend, gbuf.at[0, y], feed_send.at[0], feed_recv.at[0], device(0))
        gram_feed.wait_recv()
        ring_start(GRAM, 0)
        cross_feed.wait_recv()
        step, threshold = step_of(0)
        beta_zero = soften(step * cross_fit[0], threshold)
        bsend[0, 0] = beta_zero.astype(BF16)
        pieces_start(0, 0)
        for r in (1, 0):
            pieces_wait(0, r)
            ring_start(BETA, r)
        for hop in (1, 2, 3):
            for r in (1, 0):
                ring_step(GRAM, r, hop)
            for r in (1, 0):
                ring_step(BETA, r, hop)
        for r in (1, 0):
            ring_step(GRAM, r, 4)
            ring_step(BETA, r, 4)
            add_products(0, r, range(RING), first=True)
            start(part_copy(0, r))
        betas = [beta_zero, beta_one]
        for r in (1, 0):
            betas[r] = next_beta(0, r, betas[r])
            bsend[1, r] = betas[r].astype(BF16)
            pieces_start(1, r)
        beta_keep[...] = betas[0]
        start(remote(beta_keep, end_beta, end_send.at[2], end_recv.at[2], device(0)))
        for r in (1, 0):
            pieces_wait(1, r)
            ring_start(BETA + 1, r)
        for hop in (1, 2, 3):
            for r in (1, 0):
                ring_step(BETA + 1, r, hop)
            for r in (1, 0):
                if hop == 1:
                    add_products(1, r, (0,), first=True)
                else:
                    add_products(1, r, (hop - 1, RING + 1 - hop))
        ring_step(BETA + 1, 1, 4)
        add_products(1, 1, (3, 5, 4))
        start(part_copy(1, 1))
        ring_step(BETA + 1, 0, 4)
        add_products(1, 0, (3, 5, 4))
        start(remote(acc.at[1, 0, own_half(1 - xl)], end_part.at[1], end_send.at[1], end_recv.at[1],
                     device(0, lo=1 - xl)))
        start(remote(acc.at[1, 0, own_half(xl)], end_part.at[0], end_send.at[0], end_recv.at[0], device(0)))
        coef_out[...] = next_beta(1, 1, betas[1])

        for copy in sent:
            copy.wait_send()
        for it in range(2):
            for r in range(2):
                @pl.when(jnp.logical_not(own_k))
                def _():
                    piece_near(it, r).wait_send()

    @pl.when(c == 0)
    def _():
        COLS, ROWS = 0, 1
        row0 = pl.multiple_of(xl * 192, 16)
        row0_other = pl.multiple_of((1 - xl) * 192, 16)
        part_h, part_q = y // 4, y % 4
        rows_h = pl.multiple_of(xl * 192 + part_h * 96, 16)

        def at96(index):
            return pl.ds(pl.multiple_of(index * 96, 16), 96)

        def expr_cols(index):
            return pl.ds(pl.multiple_of(index * 512 + part_q * 128, 128), 128)

        loads = [
            load(3, gram_hbm, gram_state), load(2, cross_hbm, cross_state), load(4, target_hbm, target),
            load(0, step_hbm, step_size), load(1, penalty_hbm, penalty), load(5, subsample_hbm, subsample),
        ]
        peers = [device(0, zz=(z + d) % RING) for d in range(1, RING)]
        peers += [device(0, yy=(y + d) % RING) for d in (1, 7)]
        peers += [chip_x(right, 0), chip_x(left, 0), chip_x(right, 1), chip_x(left, 1), device(1)]
        greet(peers)
        local = [
            pltpu.make_async_copy(
                expr.at[pl.ds(pl.multiple_of(row0 + h * 96, 16), 96), pl.ds(pl.multiple_of(y * 512, 512), 512)],
                cbuf.at[h, z, :, pl.ds(0, 512)], local_sem.at[h])
            for h in range(2)
        ]
        local.append(pltpu.make_async_copy(
            expr.at[pl.ds(rows_h, 96), expr_cols(z)], rbuf.at[y, at96(z)], local_sem.at[2]))
        for copy in local:
            copy.start()
        sent = []

        def start(copy):
            copy.start()
            sent.append(copy)

        def view_of(ring, part, chunk):
            if ring == COLS:
                return cbuf.at[part, chunk]
            return rbuf.at[chunk, pl.ds(part * 384, 384)]

        ring_start, ring_step = rings(0, view_of, (ROWS,), sent)

        loads[0].wait()
        gsend[...] = gram_state[0].astype(BF16)
        loads[1].wait()
        loads[2].wait()
        both = jnp.concatenate([target[...], target[...]], axis=0)
        lane_half = lax.broadcasted_iota(jnp.int32, both.shape, 0) // 64
        both = jnp.where(lane_half == xl, both, jnp.zeros_like(both))
        tpad[...] = both.T
        tsend[...] = tpad[pl.ds(row0_other, 192), :]
        pl.semaphore_wait(barrier, len(peers))

        start(remote(gsend, gbuf.at[0, y], feed_send.at[0], feed_recv.at[0], device(1)))
        start(remote(cross_state.at[0], cross_fit.at[0], feed_send.at[1], feed_recv.at[1], device(1)))
        swap = remote(tsend, trecv, swap_send, swap_recv, device(0, lo=1 - xl))
        start(swap)
        for d in range(1, RING):
            to = (z + d) % RING
            start(remote(expr.at[pl.ds(rows_h, 96), expr_cols(to)], rbuf.at[y, at96(z)],
                         spread_send.at[d - 1], spread_recv.at[d - 1], device(0, zz=to)))
        swap.wait_recv()
        for h in range(2):
            cbuf[h, z, :, 512:640] = (
                tpad[pl.ds(pl.multiple_of(row0 + h * 96, 16), 96), :] + trecv[h * 96:(h + 1) * 96, :])
        for copy in local:
            copy.wait()
        for part in range(2):
            ring_start(COLS, part)
        for d in range(1, RING):
            source = (z + RING - d) % RING
            remote(expr.at[pl.ds(rows_h, 96), expr_cols(z)], rbuf.at[y, at96(source)],
                   spread_send.at[d - 1], spread_recv.at[d - 1], device(0, zz=source)).wait_recv()
        for part in range(2):
            ring_start(ROWS, part)

        for copy in loads[3:]:
            copy.wait()
        first_lane = xh * 384 + xl * 192
        lane = lax.broadcasted_iota(jnp.int32, (2, 768), 1)
        for h in range(2):
            weights = jnp.zeros((2, 768), F32)
            for zz in range(RING):
                cells = subsample[:, zz * 768:(zz + 1) * 768].astype(F32)
                moved = pltpu.roll(cells, (1536 + zz * 96 - h * 96 - first_lane) % 768, axis=1)
                weights = jnp.where((lane >= zz * 96) & (lane < zz * 96 + 96), moved, weights)
            wbuf[h] = weights

        def weigh(distance):
            chunk = (y + distance) % RING
            h, q = chunk // 4, chunk % 4
            block = rbuf[chunk].T
            rows = pl.ds(pl.multiple_of(q * 128, 128), 128)
            pair = wbuf[h].astype(BF16)
            for r in range(2):
                lhs[r, h, rows, :] = block * pair[r:r + 1, :]

        weigh(0)
        for hop in (1, 2, 3):
            for part in range(2):
                ring_step(ROWS, part, hop)
            for part in range(2):
                ring_step(COLS, part, hop)
            weigh(hop)
            weigh(RING - hop)
        for part in range(2):
            ring_step(COLS, part, 4)
        for h in range(2):
            tgt_t[h] = cbuf[h, :, :, 512:640].reshape(768, 128).T
        for part in range(2):
            ring_step(ROWS, part, 4)
        weigh(4)

        def sums_of(r, index):
            hi, lo = index // 2, index % 2
            gram = jnp.zeros((256, 256), F32)
            crosses = jnp.zeros((64, 256), F32)
            for h in range(2):
                rows = lhs[r, h, pl.ds(pl.multiple_of(hi * 256, 256), 256), :]
                cols = cbuf[h, :, :, pl.ds(pl.multiple_of(lo * 256, 256), 256)].reshape(768, 256)
                gram += jnp.dot(rows, cols, preferred_element_type=F32)
                crosses += lax.dot_general(
                    tgt_t[h, pl.ds(pl.multiple_of(lo * 64, 64), 64), :], rows, ROWS_T, preferred_element_type=F32)
            return gram, crosses

        top, low = pl.ds(0, 160), pl.ds(160, 160)

        def far_copy(r, half):
            rows = low if half else top
            return remote(xsend.at[r, 0, rows], xpass.at[r, rows], far_send.at[r, half], far_recv.at[r, half],
                          chip_x(left if half else right, 0))

        def near_copy(r, way, half):
            rows = low if half else top
            return remote(xsend.at[r, 1 + way, rows], xrecv.at[way, rows], near_send.at[r, way, half],
                          near_recv.at[way, half], chip_x(left if way else right, r))

        for r in (1, 0):
            gram, crosses = sums_of(r, (x + 2) % 4)
            xsend[r, 0, 0:256, :] = gram.astype(BF16)
            xsend[r, 0, 256:320, :] = crosses.astype(BF16)
            start(far_copy(r, 0))
            start(far_copy(r, 1))
        for r in (1, 0):
            gram, crosses = sums_of(r, right)
            xsend[r, 1, 160:256, :] = gram[160:256].astype(BF16)
            xsend[r, 1, 256:320, :] = crosses.astype(BF16)
            start(near_copy(r, 0, 1))
            far_copy(r, 0).wait_recv()
            xsend[r, 1, 0:160, :] = (gram[0:160] + xpass[r, 0:160, :].astype(F32)).astype(BF16)
            start(near_copy(r, 0, 0))
            gram, crosses = sums_of(r, left)
            xsend[r, 2, 0:160, :] = gram[0:160].astype(BF16)
            start(near_copy(r, 1, 0))
            far_copy(r, 1).wait_recv()
            xsend[r, 2, 160:256, :] = (gram[160:256] + xpass[r, 160:256, :].astype(F32)).astype(BF16)
            xsend[r, 2, 256:320, :] = (crosses + xpass[r, 256:320, :].astype(F32)).astype(BF16)
            start(near_copy(r, 1, 1))
        gram, crosses = sums_of(1, x)
        xsend_own = own_block.at[1]
        own_block[1, 0:256, :] = gram
        own_block[1, 256:320, :] = crosses
        start(remote(xsend_own, own_block.at[0], own_send, own_recv, device(1)))
        gram, crosses = sums_of(0, x)
        own_block[0, 0:256, :] = gram
        own_block[0, 256:320, :] = crosses

        for i in range(3):
            remote(end_beta, end_beta if i == 2 else end_part.at[i], end_send.at[i], end_recv.at[i],
                   device(1)).wait_recv()
        step = step_size[0]
        product = end_part[0] + end_part[1]
        coef_out[...] = soften(end_beta[...] - step * (product - cross_state[0]), step * penalty[0])
        for copy in sent:
            copy.wait_send()

    @pl.when(c == 1)
    def _():
        remote(own_block.at[1], own_block.at[0], own_send, own_recv, device(0)).wait_recv()

    for way in range(2):
        for half in range(2):
            rows = pl.ds(160 * half, 160)
            remote(xsend.at[0, 1 + way, rows], xrecv.at[way, rows], near_send.at[0, way, half],
                   near_recv.at[way, half], chip_x(left if way else right, 0)).wait_recv()
    sums = own_block[0] + xrecv[0].astype(F32) + xrecv[1].astype(F32)
    gram_out[...] = gram_state[1] + sums[0:256] / CELLS
    cross_out[...] = cross_state[1] + sums[256:320] / CELLS


def copy_out(gram, cross, coef, gram_out, cross_out, coef_out, gram_here, cross_here, coef_here, sems_in, sems_out):
    stages = ((gram, gram_here, gram_out), (cross, cross_here, cross_out), (coef, coef_here, coef_out))
    ins = [pltpu.make_async_copy(source, here, sems_in.at[i]) for i, (source, here, _) in enumerate(stages)]
    outs = [pltpu.make_async_copy(here, out, sems_out.at[i]) for i, (_, here, out) in enumerate(stages)]
    for copy in ins:
        copy.start()
    for arrived, copy in zip(ins, outs):
        arrived.wait()
        copy.start()
    for copy in outs:
        copy.wait()


def body(expr_stretch, target_stretch, subsample, gram_state, cross_state, step_size, penalty):
    vmem = pl.BlockSpec(memory_space=pltpu.VMEM)
    hbm = pl.BlockSpec(memory_space=pltpu.HBM)
    dma = pltpu.SemaphoreType.DMA
    out_shape = (
        jax.ShapeDtypeStruct((256, 256), F32),
        jax.ShapeDtypeStruct((64, 256), F32),
        jax.ShapeDtypeStruct((64, 256), F32),
    )
    results = pl.pallas_call(
        kernel,
        out_shape=out_shape,
        in_specs=[hbm] * 7,
        out_specs=(vmem, vmem, vmem),
        scratch_shapes=[
            pltpu.VMEM((64, 384), BF16),
            pltpu.VMEM((2, CELLS), jnp.int32),
            pltpu.VMEM((2, 256, 256), F32),
            pltpu.VMEM((2, 64, 256), F32),
            pltpu.SMEM((2,), F32),
            pltpu.SMEM((2,), F32),
            pltpu.VMEM((2, RING, 256, 256), BF16),
            pltpu.VMEM((2, 2, RING, 128, 256), BF16),
            pltpu.VMEM((2, 64, 256), F32),
            pltpu.VMEM((2, 2, 64, 256), BF16),
            pltpu.VMEM((2, 2, 128, 256), F32),
            pltpu.VMEM((2, 2, 64, 256), F32),
            pltpu.VMEM((2, RING, 96, 640), BF16),
            pltpu.VMEM((RING, 768, 128), BF16),
            pltpu.VMEM((2, 2, 512, 768), BF16),
            pltpu.VMEM((384, 128), BF16),
            pltpu.VMEM((192, 128), BF16),
            pltpu.VMEM((192, 128), BF16),
            pltpu.VMEM((2, 128, 768), BF16),
            pltpu.VMEM((2, 2, 768), F32),
            pltpu.VMEM((256, 256), BF16),
            pltpu.VMEM((2, 3, 320, 256), BF16),
            pltpu.VMEM((2, 320, 256), BF16),
            pltpu.VMEM((2, 320, 256), F32),
            pltpu.VMEM((2, 320, 256), BF16),
            pltpu.VMEM((2, 64, 256), F32),
            pltpu.VMEM((64, 256), F32),
            pltpu.VMEM((64, 256), F32),
            dma((6, 2, 4)), dma((6, 2, 4)),
            dma((7,)), dma((7,)),
            dma((2, 2, 2)), dma((2, 2, 2)),
            dma((2, 2)), dma((2, 2)),
            dma((2, 2)), dma((2, 2)),
            dma((2, 2, 2)), dma((2, 2)),
            dma((2,)), dma((2,)),
            dma((3,)), dma((3,)),
            dma, dma,
            dma, dma,
            dma((3,)),
            dma((6,)),
        ],
        compiler_params=pltpu.CompilerParams(
            collective_id=0, has_side_effects=True, vmem_limit_bytes=60 * 2**20),
    )(
        expr_stretch,
        target_stretch.T,
        subsample,
        gram_state[:, 0],
        jnp.swapaxes(cross_state[:, 0], 1, 2),
        step_size,
        penalty,
    )
    gram, cross, coef = pl.pallas_call(
        copy_out,
        out_shape=out_shape,
        in_specs=[hbm] * 3,
        out_specs=(hbm, hbm, hbm),
        scratch_shapes=[
            pltpu.VMEM((256, 256), F32),
            pltpu.VMEM((64, 256), F32),
            pltpu.VMEM((64, 256), F32),
            dma((3,)),
            dma((3,)),
        ],
        compiler_params=pltpu.CompilerParams(vmem_limit_bytes=60 * 2**20),
    )(*results)
    return gram[None], cross.T[None], coef.T[None]


def solution(mesh):
    return jax.shard_map(
        body,
        mesh=mesh,
        in_specs=(
            P("reg", None),
            P("reg", "tgt"),
            P(),
            P(None, "grp", "reg", "tgt"),
            P(None, "grp", "reg", "tgt"),
            P(),
            P(),
        ),
        out_specs=(P("grp", "reg", "tgt"), P("grp", "reg", "tgt"), P("grp", "reg", "tgt")),
        check_vma=False,
    )
```

time: 440 us -> 58.9 us (0.13)
  waiting for transfers between devices: 323 us -> 0 us
  Pallas kernels: 0 us -> 58.1 us
  blocking collectives: 54.5 us -> 0 us
  starting transfers between devices: 19.9 us -> 0 us
  local copies, waits for them, and re-layouts: 13.7 us -> 0 us
  between operations: 14 us -> 0.64 us
  other arithmetic: 7.68 us -> 0 us
  matrix products: 6.63 us -> 0 us
    all_gather x4 -> x0, waiting for transfers between devices: 309 us -> none  [the longest x2 159 us: fit_lasso(): shard_piece = lax.all_gather(beta_low, 'reg', axis=1, tiled=True)]
    pallas_call x0 -> x2, Pallas kernels: none -> 58.1 us  [the longest x1 56.4 us: body(): pl.pallas_call(kernel, out_shape=out_shape, in_specs=[hbm] * 7, out_specs...]
    all_gather x1 -> x0, blocking collectives: 54.5 us -> none  [body(): lax.all_gather(target_stretch, 'reg', axis=0, tiled=True)]
    ppermute x3 -> x0, waiting for transfers between devices: 14.4 us -> none  [the longest x2 14.4 us: from_behind(): return lax.ppermute(block, axis, route)]
    ppermute x3 -> x0, starting transfers between devices: 12.6 us -> none  [the longest x1 8.78 us: partner(): return lax.ppermute(value, axis, pairs)]
    all_to_all x1 -> x0, starting transfers between devices: 7.23 us -> none  [body(): lax.all_to_all(expr_stretch, 'reg', split_axis=1, concat_axis=0, tiled=True)]
    unnamed x16 -> x0, local copies, waits for them, and re-layouts: 6.7 us -> none
    dot_general x2 -> x0, matrix products: 6.63 us -> none  [add_accumulate(): jnp.einsum('rak,rkb->rab', gram_whole, shard_piece, preferred_element_typ...]
  transfers between devices with their start and end apart: 8 -> 0, of which waited for: 5 -> 0; matrix products, arithmetic and copies ran while one was open for 4% -> 0% of each run, Pallas kernels for 0% -> 0%
where the time goes in v1:
time: 58.9 us; the launch traced here: 58.8 us
  Pallas kernels  58.1 us (99%)
  between operations  0.64 us (1%)
    pallas_call x1, Pallas kernels, body(): pl.pallas_call(kernel, out_shape=out_shape, in_specs=[hbm] * 7, out_specs...  56.4 us
    pallas_call x1, Pallas kernels, body(): pl.pallas_call(copy_out, out_shape=out_shape, in_specs=[hbm] * 3, out_spe...  1.74 us

profile of v1, /device:TPU:1, one launch (start us, length us, event | category | flops | bytes accessed | tf_op | source)
XLA Modules:
  0.0 58.8 jit_solution(12714136891661260315)
XLA Ops:
  0.6 56.4 %shard_map.94 = (f32[256,256]{1,0:T(8,128)}, f32[64,256]{1,0:T(8,128)}, f32[64,256]{1,0:T(8,128)}) custom-call(bf16[384,4096]{1,0:T(8,128)(2,1)} %expr.1, bf16[64,384]{1,0:T(8,128)(2,1)} %bitcast.14, s32[2,6144]{1,0:T(2,128)} %subsample_hbm.1, f32[2,256,256]{2,1,0:T(8,128)} %bitcast.12, f32[2,64,256]{2,1,0:T(8,128)} %bitcast.13, f32[2]{0:T(128)} %step_hbm.1, ...), custom_call_target="tpu_custom_call" | custom-call | tf_op jit(solution)/shard_map/pallas_call | solution.py:450
  57.0 1.7 %shard_map.95 = (f32[256,256]{1,0:T(8,128)}, f32[64,256]{1,0:T(8,128)}, f32[64,256]{1,0:T(8,128)}) custom-call(f32[256,256]{1,0:T(8,128)} %get-tuple-element.9.gram, f32[64,256]{1,0:T(8,128)} %get-tuple-element.10.cross, f32[64,256]{1,0:T(8,128)} %get-tuple-element.11.coef), custom_call_target="tpu_custom_call" | custom-call | tf_op jit(solution)/shard_map/pallas_call | solution.py:508

commit v2 on v1

--- a/solution.py
+++ b/solution.py
@@ -20,7 +20,7 @@
     gram_out, cross_out, coef_out,
     target, subsample, gram_state, cross_state, step_size, penalty,
     gbuf, bbuf, cross_fit, bsend, acc, precv,
-    cbuf, rbuf, lhs, tpad, tsend, trecv, tgt_t, wbuf, gsend,
+    cbuf, tbuf, rbuf, lhs, tpad, tsend, trecv, crosses, wbuf, gsend,
     xsend, xpass, own_block, xrecv, end_part, end_beta, beta_keep,
     ring_send, ring_recv, spread_send, spread_recv, piece_send, piece_recv,
     part_send, part_recv, far_send, far_recv, near_send, near_recv,
@@ -184,17 +184,25 @@
         bsend[0, 0] = beta_zero.astype(BF16)
         pieces_start(0, 0)
         for r in (1, 0):
+            ring_step(GRAM, r, 1)
             pieces_wait(0, r)
             ring_start(BETA, r)
-        for hop in (1, 2, 3):
-            for r in (1, 0):
-                ring_step(GRAM, r, hop)
+        for r in (1, 0):
+            ring_step(BETA, r, 1)
+        for r in (1, 0):
+            ring_step(GRAM, r, 2)
+        for r in (1, 0):
+            ring_step(BETA, r, 2)
+        for r in (1, 0):
+            ring_step(GRAM, r, 3)
+        for hop in (3, 4):
             for r in (1, 0):
                 ring_step(BETA, r, hop)
         for r in (1, 0):
+            add_products(0, r, (0, 1, 2, 3, 5, 6, 7), first=True)
+        for r in (1, 0):
             ring_step(GRAM, r, 4)
-            ring_step(BETA, r, 4)
-            add_products(0, r, range(RING), first=True)
+            add_products(0, r, (4,))
             start(part_copy(0, r))
         betas = [beta_zero, beta_one]
         for r in (1, 0):
@@ -234,7 +242,7 @@
 
     @pl.when(c == 0)
     def _():
-        COLS, ROWS = 0, 1
+        COLS, ROWS, TARGETS = 0, 1, 2
         row0 = pl.multiple_of(xl * 192, 16)
         row0_other = pl.multiple_of((1 - xl) * 192, 16)
         part_h, part_q = y // 4, y % 4
@@ -257,7 +265,7 @@
         local = [
             pltpu.make_async_copy(
                 expr.at[pl.ds(pl.multiple_of(row0 + h * 96, 16), 96), pl.ds(pl.multiple_of(y * 512, 512), 512)],
-                cbuf.at[h, z, :, pl.ds(0, 512)], local_sem.at[h])
+                cbuf.at[h, z], local_sem.at[h])
             for h in range(2)
         ]
         local.append(pltpu.make_async_copy(
@@ -273,6 +281,8 @@
         def view_of(ring, part, chunk):
             if ring == COLS:
                 return cbuf.at[part, chunk]
+            if ring == TARGETS:
+                return tbuf.at[chunk]
             return rbuf.at[chunk, pl.ds(part * 384, 384)]
 
         ring_start, ring_step = rings(0, view_of, (ROWS,), sent)
@@ -296,14 +306,15 @@
             to = (z + d) % RING
             start(remote(expr.at[pl.ds(rows_h, 96), expr_cols(to)], rbuf.at[y, at96(z)],
                          spread_send.at[d - 1], spread_recv.at[d - 1], device(0, zz=to)))
-        swap.wait_recv()
-        for h in range(2):
-            cbuf[h, z, :, 512:640] = (
-                tpad[pl.ds(pl.multiple_of(row0 + h * 96, 16), 96), :] + trecv[h * 96:(h + 1) * 96, :])
         for copy in local:
             copy.wait()
         for part in range(2):
             ring_start(COLS, part)
+        swap.wait_recv()
+        for h in range(2):
+            tbuf[z, h] = (
+                tpad[pl.ds(pl.multiple_of(row0 + h * 96, 16), 96), :] + trecv[h * 96:(h + 1) * 96, :])
+        ring_start(TARGETS, 0)
         for d in range(1, RING):
             source = (z + RING - d) % RING
             remote(expr.at[pl.ds(rows_h, 96), expr_cols(z)], rbuf.at[y, at96(source)],
@@ -338,27 +349,37 @@
                 ring_step(ROWS, part, hop)
             for part in range(2):
                 ring_step(COLS, part, hop)
+            ring_step(TARGETS, 0, hop)
             weigh(hop)
             weigh(RING - hop)
         for part in range(2):
             ring_step(COLS, part, 4)
-        for h in range(2):
-            tgt_t[h] = cbuf[h, :, :, 512:640].reshape(768, 128).T
+        ring_step(TARGETS, 0, 4)
         for part in range(2):
             ring_step(ROWS, part, 4)
         weigh(4)
 
-        def sums_of(r, index):
+        def rows_of(hi, h):
+            half = pl.ds(pl.multiple_of(hi * 256, 256), 256)
+            return jnp.concatenate([lhs[0, h, half, :], lhs[1, h, half, :]], axis=0)
+
+        def grams_of(index):
             hi, lo = index // 2, index % 2
-            gram = jnp.zeros((256, 256), F32)
-            crosses = jnp.zeros((64, 256), F32)
+            total = jnp.zeros((512, 256), F32)
             for h in range(2):
-                rows = lhs[r, h, pl.ds(pl.multiple_of(hi * 256, 256), 256), :]
                 cols = cbuf[h, :, :, pl.ds(pl.multiple_of(lo * 256, 256), 256)].reshape(768, 256)
-                gram += jnp.dot(rows, cols, preferred_element_type=F32)
-                crosses += lax.dot_general(
-                    tgt_t[h, pl.ds(pl.multiple_of(lo * 64, 64), 64), :], rows, ROWS_T, preferred_element_type=F32)
-            return gram, crosses
+                total += jnp.dot(rows_of(hi, h), cols, preferred_element_type=F32)
+            return total[0:256], total[256:512]
+
+        def make_crosses(hi):
+            total = jnp.zeros((512, 128), F32)
+            for h in range(2):
+                total += jnp.dot(rows_of(hi, h), tbuf[:, h].reshape(768, 128), preferred_element_type=F32)
+            for r in range(2):
+                crosses[hi, r] = total[r * 256:(r + 1) * 256].T
+
+        def crosses_of(r, index):
+            return crosses[index // 2, r, pl.ds(pl.multiple_of((index % 2) * 64, 64), 64), :]
 
         top, low = pl.ds(0, 160), pl.ds(160, 160)
 
@@ -372,35 +393,38 @@
             return remote(xsend.at[r, 1 + way, rows], xrecv.at[way, rows], near_send.at[r, way, half],
                           near_recv.at[way, half], chip_x(left if way else right, r))
 
-        for r in (1, 0):
-            gram, crosses = sums_of(r, (x + 2) % 4)
-            xsend[r, 0, 0:256, :] = gram.astype(BF16)
-            xsend[r, 0, 256:320, :] = crosses.astype(BF16)
+        far = (x + 2) % 4
+        make_crosses(1 - xh)
+        grams = grams_of(far)
+        for r in (1, 0):
+            xsend[r, 0, 0:256, :] = grams[r].astype(BF16)
+            xsend[r, 0, 256:320, :] = crosses_of(r, far).astype(BF16)
             start(far_copy(r, 0))
             start(far_copy(r, 1))
-        for r in (1, 0):
-            gram, crosses = sums_of(r, right)
-            xsend[r, 1, 160:256, :] = gram[160:256].astype(BF16)
-            xsend[r, 1, 256:320, :] = crosses.astype(BF16)
+        make_crosses(xh)
+        grams_right = grams_of(right)
+        for r in (1, 0):
+            xsend[r, 1, 160:256, :] = grams_right[r][160:256].astype(BF16)
+            xsend[r, 1, 256:320, :] = crosses_of(r, right).astype(BF16)
             start(near_copy(r, 0, 1))
+        grams_left = grams_of(left)
+        for r in (1, 0):
+            xsend[r, 2, 0:160, :] = grams_left[r][0:160].astype(BF16)
+            start(near_copy(r, 1, 0))
+        for r in (1, 0):
             far_copy(r, 0).wait_recv()
-            xsend[r, 1, 0:160, :] = (gram[0:160] + xpass[r, 0:160, :].astype(F32)).astype(BF16)
+            xsend[r, 1, 0:160, :] = (grams_right[r][0:160] + xpass[r, 0:160, :].astype(F32)).astype(BF16)
             start(near_copy(r, 0, 0))
-            gram, crosses = sums_of(r, left)
-            xsend[r, 2, 0:160, :] = gram[0:160].astype(BF16)
-            start(near_copy(r, 1, 0))
             far_copy(r, 1).wait_recv()
-            xsend[r, 2, 160:256, :] = (gram[160:256] + xpass[r, 160:256, :].astype(F32)).astype(BF16)
-            xsend[r, 2, 256:320, :] = (crosses + xpass[r, 256:320, :].astype(F32)).astype(BF16)
+            xsend[r, 2, 160:256, :] = (grams_left[r][160:256] + xpass[r, 160:256, :].astype(F32)).astype(BF16)
+            xsend[r, 2, 256:320, :] = (crosses_of(r, left) + xpass[r, 256:320, :].astype(F32)).astype(BF16)
             start(near_copy(r, 1, 1))
-        gram, crosses = sums_of(1, x)
-        xsend_own = own_block.at[1]
-        own_block[1, 0:256, :] = gram
-        own_block[1, 256:320, :] = crosses
-        start(remote(xsend_own, own_block.at[0], own_send, own_recv, device(1)))
-        gram, crosses = sums_of(0, x)
-        own_block[0, 0:256, :] = gram
-        own_block[0, 256:320, :] = crosses
+        grams = grams_of(x)
+        own_block[1, 0:256, :] = grams[1]
+        own_block[1, 256:320, :] = crosses_of(1, x)
+        start(remote(own_block.at[1], own_block.at[0], own_send, own_recv, device(1)))
+        own_block[0, 0:256, :] = grams[0]
+        own_block[0, 256:320, :] = crosses_of(0, x)
 
         for i in range(3):
             remote(end_beta, end_beta if i == 2 else end_part.at[i], end_send.at[i], end_recv.at[i],
@@ -465,13 +489,14 @@
             pltpu.VMEM((2, 2, 64, 256), BF16),
             pltpu.VMEM((2, 2, 128, 256), F32),
             pltpu.VMEM((2, 2, 64, 256), F32),
-            pltpu.VMEM((2, RING, 96, 640), BF16),
+            pltpu.VMEM((2, RING, 96, 512), BF16),
+            pltpu.VMEM((RING, 2, 96, 128), BF16),
             pltpu.VMEM((RING, 768, 128), BF16),
             pltpu.VMEM((2, 2, 512, 768), BF16),
             pltpu.VMEM((384, 128), BF16),
             pltpu.VMEM((192, 128), BF16),
             pltpu.VMEM((192, 128), BF16),
-            pltpu.VMEM((2, 128, 768), BF16),
+            pltpu.VMEM((2, 2, 128, 256), F32),
             pltpu.VMEM((2, 2, 768), F32),
             pltpu.VMEM((256, 256), BF16),
             pltpu.VMEM((2, 3, 320, 256), BF16),

time: 58.9 us -> 58.9 us (level)
  no operation moved by 1% of the time
where the time goes in v2:
time: 58.9 us; the launch traced here: 58.8 us
  Pallas kernels  58.1 us (99%)
  between operations  0.64 us (1%)
    pallas_call x1, Pallas kernels, body(): pl.pallas_call(kernel, out_shape=out_shape, in_specs=[hbm] * 7, out_specs...  56.4 us
    pallas_call x1, Pallas kernels, body(): pl.pallas_call(copy_out, out_shape=out_shape, in_specs=[hbm] * 3, out_spe...  1.74 us

profile of v2, /device:TPU:1, one launch (start us, length us, event | category | flops | bytes accessed | tf_op | source)
XLA Modules:
  0.0 58.8 jit_solution(13723538769900023258)
XLA Ops:
  0.6 56.4 %shard_map.94 = (f32[256,256]{1,0:T(8,128)}, f32[64,256]{1,0:T(8,128)}, f32[64,256]{1,0:T(8,128)}) custom-call(bf16[384,4096]{1,0:T(8,128)(2,1)} %expr.1, bf16[64,384]{1,0:T(8,128)(2,1)} %bitcast.14, s32[2,6144]{1,0:T(2,128)} %subsample_hbm.1, f32[2,256,256]{2,1,0:T(8,128)} %bitcast.12, f32[2,64,256]{2,1,0:T(8,128)} %bitcast.13, f32[2]{0:T(128)} %step_hbm.1, ...), custom_call_target="tpu_custom_call" | custom-call | tf_op jit(solution)/shard_map/pallas_call | solution.py:474
  57.0 1.7 %shard_map.95 = (f32[256,256]{1,0:T(8,128)}, f32[64,256]{1,0:T(8,128)}, f32[64,256]{1,0:T(8,128)}) custom-call(f32[256,256]{1,0:T(8,128)} %get-tuple-element.9.gram, f32[64,256]{1,0:T(8,128)} %get-tuple-element.10.cross, f32[64,256]{1,0:T(8,128)} %get-tuple-element.11.coef), custom_call_target="tpu_custom_call" | custom-call | tf_op jit(solution)/shard_map/pallas_call | solution.py:533

commit v3 on v2

--- a/solution.py
+++ b/solution.py
@@ -20,12 +20,12 @@
     gram_out, cross_out, coef_out,
     target, subsample, gram_state, cross_state, step_size, penalty,
     gbuf, bbuf, cross_fit, bsend, acc, precv,
-    cbuf, tbuf, rbuf, lhs, tpad, tsend, trecv, crosses, wbuf, gsend,
+    bsend_zero, cbuf, tbuf, rbuf, lhs, tpad, tsend, trecv, crosses, wbuf, gsend,
     xsend, xpass, own_block, xrecv, end_part, end_beta, beta_keep,
     ring_send, ring_recv, spread_send, spread_recv, piece_send, piece_recv,
     part_send, part_recv, far_send, far_recv, near_send, near_recv,
     feed_send, feed_recv, end_send, end_recv, own_send, own_recv,
-    swap_send, swap_recv, local_sem, load_sem,
+    swap_send, swap_recv, local_sem, load_sem, first_send, reach_send, reach_recv,
 ):
     c = lax.axis_index("grp")
     reg = lax.axis_index("reg")
@@ -88,6 +88,16 @@
 
         return ring_start, ring_step
 
+    def finish_sums():
+        for way in range(2):
+            for half in range(2):
+                rows = pl.ds(160 * half, 160)
+                remote(xsend.at[0, 1 + way, rows], xrecv.at[way, rows], near_send.at[0, way, half],
+                       near_recv.at[way, half], chip_x(left if way else right, 0)).wait_recv()
+        sums = own_block[0] + xrecv[0].astype(F32) + xrecv[1].astype(F32)
+        gram_out[...] = gram_state[1] + sums[0:256] / CELLS
+        cross_out[...] = cross_state[1] + sums[256:320] / CELLS
+
     @pl.when(c == 1)
     def _():
         GRAM, BETA = 0, 1
@@ -95,10 +105,10 @@
             load(0, step_hbm, step_size), load(1, penalty_hbm, penalty),
             load(2, cross_hbm, cross_state), load(3, gram_hbm, gram_state),
         ]
-        peers = [device(1, zz=(z + d) % RING) for d in (1, 7)]
-        peers += [device(1, yy=(y + d) % RING) for d in (1, 7)]
-        peers += [chip_x((x + d) % 4, 1) for d in (1, 2, 3)]
-        peers += [chip_x(right, 0), chip_x(left, 0), device(0)]
+        peers = [device(1, zz=(z + d) % RING) for d in (1, 2, 6, 7)]
+        peers += [device(core, yy=(y + d) % RING) for core in (0, 1) for d in (1, 7)]
+        peers += [chip_x((x + d) % 4, core) for core in (0, 1) for d in (1, 2, 3)]
+        peers += [device(0)]
         greet(peers)
         sent = []
 
@@ -176,13 +186,6 @@
         pieces_start(0, 1)
         cross_feed = remote(cross_state.at[0], cross_fit.at[0], feed_send.at[1], feed_recv.at[1], device(0))
         gram_feed = remote(gsend, gbuf.at[0, y], feed_send.at[0], feed_recv.at[0], device(0))
-        gram_feed.wait_recv()
-        ring_start(GRAM, 0)
-        cross_feed.wait_recv()
-        step, threshold = step_of(0)
-        beta_zero = soften(step * cross_fit[0], threshold)
-        bsend[0, 0] = beta_zero.astype(BF16)
-        pieces_start(0, 0)
         for r in (1, 0):
             ring_step(GRAM, r, 1)
             pieces_wait(0, r)
@@ -198,6 +201,10 @@
         for hop in (3, 4):
             for r in (1, 0):
                 ring_step(BETA, r, hop)
+        cross_feed.wait_recv()
+        step, threshold = step_of(0)
+        beta_zero = soften(step * cross_fit[0], threshold)
+        gram_feed.wait_recv()
         for r in (1, 0):
             add_products(0, r, (0, 1, 2, 3, 5, 6, 7), first=True)
         for r in (1, 0):
@@ -211,34 +218,56 @@
             pieces_start(1, r)
         beta_keep[...] = betas[0]
         start(remote(beta_keep, end_beta, end_send.at[2], end_recv.at[2], device(0)))
+        def reach_copy(r, slot, chunk, to):
+            view = bbuf.at[1, r, chunk % RING]
+            return remote(view, view, reach_send.at[r, slot], reach_recv.at[r, slot],
+                          device(1, zz=(z + to) % RING))
+
+        M1, P1, M2, P2, M3, P3, FAR = range(7)
         for r in (1, 0):
             pieces_wait(1, r)
-            ring_start(BETA + 1, r)
-        for hop in (1, 2, 3):
-            for r in (1, 0):
-                ring_step(BETA + 1, r, hop)
-            for r in (1, 0):
-                if hop == 1:
-                    add_products(1, r, (0,), first=True)
-                else:
-                    add_products(1, r, (hop - 1, RING + 1 - hop))
-        ring_step(BETA + 1, 1, 4)
-        add_products(1, 1, (3, 5, 4))
+            start(reach_copy(r, M2, z, 2))
+            start(reach_copy(r, P2, z, 6))
+            start(reach_copy(r, M1, z, 1))
+            start(reach_copy(r, P1, z, 7))
+        for r in (1, 0):
+            add_products(1, r, (0,), first=True)
+        for r in (1, 0):
+            reach_copy(r, M2, z + 6, 2).wait_recv()
+            start(reach_copy(r, M3, z + 6, 1))
+            if r == 0:
+                start(reach_copy(r, FAR, z + 6, 2))
+            reach_copy(r, P2, z + 2, 6).wait_recv()
+            start(reach_copy(r, P3, z + 2, 7))
+            if r == 1:
+                start(reach_copy(r, FAR, z + 2, 6))
+        for r in (1, 0):
+            reach_copy(r, M1, z + 7, 1).wait_recv()
+            reach_copy(r, P1, z + 1, 7).wait_recv()
+            add_products(1, r, (1, 2, 6, 7))
+
+        def last_products(r):
+            reach_copy(r, M3, z + 5, 1).wait_recv()
+            reach_copy(r, P3, z + 3, 7).wait_recv()
+            reach_copy(r, FAR, z + 4, 2).wait_recv()
+            add_products(1, r, (3, 4, 5))
+
+        last_products(1)
         start(part_copy(1, 1))
-        ring_step(BETA + 1, 0, 4)
-        add_products(1, 0, (3, 5, 4))
+        last_products(0)
         start(remote(acc.at[1, 0, own_half(1 - xl)], end_part.at[1], end_send.at[1], end_recv.at[1],
                      device(0, lo=1 - xl)))
         start(remote(acc.at[1, 0, own_half(xl)], end_part.at[0], end_send.at[0], end_recv.at[0], device(0)))
+        remote(own_block.at[1], own_block.at[0], own_send, own_recv, device(0)).wait_recv()
+        finish_sums()
         coef_out[...] = next_beta(1, 1, betas[1])
 
         for copy in sent:
             copy.wait_send()
-        for it in range(2):
-            for r in range(2):
-                @pl.when(jnp.logical_not(own_k))
-                def _():
-                    piece_near(it, r).wait_send()
+        for it, r in ((0, 1), (1, 0), (1, 1)):
+            @pl.when(jnp.logical_not(own_k))
+            def _():
+                piece_near(it, r).wait_send()
 
     @pl.when(c == 0)
     def _():
@@ -255,12 +284,13 @@
             return pl.ds(pl.multiple_of(index * 512 + part_q * 128, 128), 128)
 
         loads = [
-            load(3, gram_hbm, gram_state), load(2, cross_hbm, cross_state), load(4, target_hbm, target),
-            load(0, step_hbm, step_size), load(1, penalty_hbm, penalty), load(5, subsample_hbm, subsample),
+            load(0, step_hbm, step_size), load(1, penalty_hbm, penalty), load(2, cross_hbm, cross_state),
+            load(3, gram_hbm, gram_state), load(4, target_hbm, target), load(5, subsample_hbm, subsample),
         ]
         peers = [device(0, zz=(z + d) % RING) for d in range(1, RING)]
-        peers += [device(0, yy=(y + d) % RING) for d in (1, 7)]
-        peers += [chip_x(right, 0), chip_x(left, 0), chip_x(right, 1), chip_x(left, 1), device(1)]
+        peers += [device(core, yy=(y + d) % RING) for core in (0, 1) for d in (1, 7)]
+        peers += [chip_x(right, 0), chip_x(left, 0), device(1)]
+        peers += [chip_x((x + d) % 4, 1) for d in (1, 2, 3)]
         greet(peers)
         local = [
             pltpu.make_async_copy(
@@ -287,10 +317,13 @@
 
         ring_start, ring_step = rings(0, view_of, (ROWS,), sent)
 
-        loads[0].wait()
+        for copy in loads[:4]:
+            copy.wait()
         gsend[...] = gram_state[0].astype(BF16)
-        loads[1].wait()
-        loads[2].wait()
+        step = step_size[0]
+        threshold = step * penalty[0]
+        bsend_zero[...] = soften(step * cross_state[0], threshold).astype(BF16)
+        loads[4].wait()
         both = jnp.concatenate([target[...], target[...]], axis=0)
         lane_half = lax.broadcasted_iota(jnp.int32, both.shape, 0) // 64
         both = jnp.where(lane_half == xl, both, jnp.zeros_like(both))
@@ -298,6 +331,12 @@
         tsend[...] = tpad[pl.ds(row0_other, 192), :]
         pl.semaphore_wait(barrier, len(peers))
 
+        for way in range(2):
+            start(remote(gsend, gbuf.at[0, y], first_send.at[way], ring_recv.at[0, way, 0],
+                         device(1, yy=(y + (7 if way else 1)) % RING)))
+        for i, hi in enumerate((1 - xh, xh)):
+            start(remote(bsend_zero, bbuf.at[0, 0, z, pl.ds(pl.multiple_of(xl * 64, 64), 64)], first_send.at[2 + i],
+                         piece_recv.at[0, 0, xl], device(1, hi=hi, lo=xh)))
         start(remote(gsend, gbuf.at[0, y], feed_send.at[0], feed_recv.at[0], device(1)))
         start(remote(cross_state.at[0], cross_fit.at[0], feed_send.at[1], feed_recv.at[1], device(1)))
         swap = remote(tsend, trecv, swap_send, swap_recv, device(0, lo=1 - xl))
@@ -322,8 +361,7 @@
         for part in range(2):
             ring_start(ROWS, part)
 
-        for copy in loads[3:]:
-            copy.wait()
+        loads[5].wait()
         first_lane = xh * 384 + xl * 192
         lane = lax.broadcasted_iota(jnp.int32, (2, 768), 1)
         for h in range(2):
@@ -426,27 +464,14 @@
         own_block[0, 0:256, :] = grams[0]
         own_block[0, 256:320, :] = crosses_of(0, x)
 
+        finish_sums()
         for i in range(3):
             remote(end_beta, end_beta if i == 2 else end_part.at[i], end_send.at[i], end_recv.at[i],
                    device(1)).wait_recv()
-        step = step_size[0]
         product = end_part[0] + end_part[1]
-        coef_out[...] = soften(end_beta[...] - step * (product - cross_state[0]), step * penalty[0])
+        coef_out[...] = soften(end_beta[...] - step * (product - cross_state[0]), threshold)
         for copy in sent:
             copy.wait_send()
-
-    @pl.when(c == 1)
-    def _():
-        remote(own_block.at[1], own_block.at[0], own_send, own_recv, device(0)).wait_recv()
-
-    for way in range(2):
-        for half in range(2):
-            rows = pl.ds(160 * half, 160)
-            remote(xsend.at[0, 1 + way, rows], xrecv.at[way, rows], near_send.at[0, way, half],
-                   near_recv.at[way, half], chip_x(left if way else right, 0)).wait_recv()
-    sums = own_block[0] + xrecv[0].astype(F32) + xrecv[1].astype(F32)
-    gram_out[...] = gram_state[1] + sums[0:256] / CELLS
-    cross_out[...] = cross_state[1] + sums[256:320] / CELLS
 
 
 def copy_out(gram, cross, coef, gram_out, cross_out, coef_out, gram_here, cross_here, coef_here, sems_in, sems_out):
@@ -489,6 +514,7 @@
             pltpu.VMEM((2, 2, 64, 256), BF16),
             pltpu.VMEM((2, 2, 128, 256), F32),
             pltpu.VMEM((2, 2, 64, 256), F32),
+            pltpu.VMEM((64, 256), BF16),
             pltpu.VMEM((2, RING, 96, 512), BF16),
             pltpu.VMEM((RING, 2, 96, 128), BF16),
             pltpu.VMEM((RING, 768, 128), BF16),
@@ -518,6 +544,8 @@
             dma, dma,
             dma((3,)),
             dma((6,)),
+            dma((4,)),
+            dma((2, 7)), dma((2, 7)),
         ],
         compiler_params=pltpu.CompilerParams(
             collective_id=0, has_side_effects=True, vmem_limit_bytes=60 * 2**20),

time: 58.9 us -> 59.3 us (level)
  no operation moved by 1% of the time
where the time goes in v3:
time: 59.3 us; the launch traced here: 59.1 us
  Pallas kernels  58.5 us (99%)
  between operations  0.64 us (1%)
    pallas_call x1, Pallas kernels, body(): pl.pallas_call(kernel, out_shape=out_shape, in_specs=[hbm] * 7, out_specs...  56.7 us
    pallas_call x1, Pallas kernels, body(): pl.pallas_call(copy_out, out_shape=out_shape, in_specs=[hbm] * 3, out_spe...  1.74 us

profile of v3, /device:TPU:1, one launch (start us, length us, event | category | flops | bytes accessed | tf_op | source)
XLA Modules:
  0.0 59.1 jit_solution(4567997873975908539)
XLA Ops:
  0.6 56.7 %shard_map.94 = (f32[256,256]{1,0:T(8,128)}, f32[64,256]{1,0:T(8,128)}, f32[64,256]{1,0:T(8,128)}) custom-call(bf16[384,4096]{1,0:T(8,128)(2,1)} %expr.1, bf16[64,384]{1,0:T(8,128)(2,1)} %bitcast.14, s32[2,6144]{1,0:T(2,128)} %subsample_hbm.1, f32[2,256,256]{2,1,0:T(8,128)} %bitcast.12, f32[2,64,256]{2,1,0:T(8,128)} %bitcast.13, f32[2]{0:T(128)} %step_hbm.1, ...), custom_call_target="tpu_custom_call" | custom-call | tf_op jit(solution)/shard_map/pallas_call | solution.py:499
  57.4 1.7 %shard_map.95 = (f32[256,256]{1,0:T(8,128)}, f32[64,256]{1,0:T(8,128)}, f32[64,256]{1,0:T(8,128)}) custom-call(f32[256,256]{1,0:T(8,128)} %get-tuple-element.9.gram, f32[64,256]{1,0:T(8,128)} %get-tuple-element.10.cross, f32[64,256]{1,0:T(8,128)} %get-tuple-element.11.coef), custom_call_target="tpu_custom_call" | custom-call | tf_op jit(solution)/shard_map/pallas_call | solution.py:561

commit v4 on v3

--- a/solution.py
+++ b/solution.py
@@ -20,12 +20,12 @@
     gram_out, cross_out, coef_out,
     target, subsample, gram_state, cross_state, step_size, penalty,
     gbuf, bbuf, cross_fit, bsend, acc, precv,
-    bsend_zero, cbuf, tbuf, rbuf, lhs, tpad, tsend, trecv, crosses, wbuf, gsend,
+    bsend_zero, stage, cbuf, tbuf, rbuf, lhs, tpad, tsend, trecv, crosses, wbuf, gsend,
     xsend, xpass, own_block, xrecv, end_part, end_beta, beta_keep,
     ring_send, ring_recv, spread_send, spread_recv, piece_send, piece_recv,
     part_send, part_recv, far_send, far_recv, near_send, near_recv,
     feed_send, feed_recv, end_send, end_recv, own_send, own_recv,
-    swap_send, swap_recv, local_sem, load_sem, first_send, reach_send, reach_recv,
+    swap_send, swap_recv, local_sem, load_sem, stage_sem, first_send, reach_send, reach_recv,
 ):
     c = lax.axis_index("grp")
     reg = lax.axis_index("reg")
@@ -283,15 +283,21 @@
         def expr_cols(index):
             return pl.ds(pl.multiple_of(index * 512 + part_q * 128, 128), 128)
 
-        loads = [
-            load(0, step_hbm, step_size), load(1, penalty_hbm, penalty), load(2, cross_hbm, cross_state),
-            load(3, gram_hbm, gram_state), load(4, target_hbm, target), load(5, subsample_hbm, subsample),
-        ]
         peers = [device(0, zz=(z + d) % RING) for d in range(1, RING)]
         peers += [device(core, yy=(y + d) % RING) for core in (0, 1) for d in (1, 7)]
         peers += [chip_x(right, 0), chip_x(left, 0), device(1)]
         peers += [chip_x((x + d) % 4, 1) for d in (1, 2, 3)]
         greet(peers)
+        loads = [
+            load(0, step_hbm, step_size), load(1, penalty_hbm, penalty), load(2, cross_hbm, cross_state),
+            load(3, gram_hbm, gram_state),
+        ]
+        stages = [
+            pltpu.make_async_copy(expr.at[pl.ds(rows_h, 96), expr_cols((z + d) % RING)], stage.at[d], stage_sem.at[d])
+            for d in range(1, RING)
+        ]
+        for copy in stages:
+            copy.start()
         local = [
             pltpu.make_async_copy(
                 expr.at[pl.ds(pl.multiple_of(row0 + h * 96, 16), 96), pl.ds(pl.multiple_of(y * 512, 512), 512)],
@@ -302,6 +308,7 @@
             expr.at[pl.ds(rows_h, 96), expr_cols(z)], rbuf.at[y, at96(z)], local_sem.at[2]))
         for copy in local:
             copy.start()
+        loads += [load(4, target_hbm, target), load(5, subsample_hbm, subsample)]
         sent = []
 
         def start(copy):
@@ -323,43 +330,43 @@
         step = step_size[0]
         threshold = step * penalty[0]
         bsend_zero[...] = soften(step * cross_state[0], threshold).astype(BF16)
+        pl.semaphore_wait(barrier, len(peers))
+
+        for way in range(2):
+            start(remote(gsend, gbuf.at[0, y], first_send.at[way], ring_recv.at[0, way, 0],
+                         device(1, yy=(y + (7 if way else 1)) % RING)))
+        for i, hi in enumerate((1 - xh, xh)):
+            start(remote(bsend_zero, bbuf.at[0, 0, z, pl.ds(pl.multiple_of(xl * 64, 64), 64)], first_send.at[2 + i],
+                         piece_recv.at[0, 0, xl], device(1, hi=hi, lo=xh)))
+        for d in range(1, RING):
+            stages[d - 1].wait()
+            start(remote(stage.at[d], rbuf.at[y, at96(z)], spread_send.at[d - 1], spread_recv.at[d - 1],
+                         device(0, zz=(z + d) % RING)))
+        for copy in local:
+            copy.wait()
+        for part in range(2):
+            ring_start(COLS, part)
+        start(remote(gsend, gbuf.at[0, y], feed_send.at[0], feed_recv.at[0], device(1)))
+        start(remote(cross_state.at[0], cross_fit.at[0], feed_send.at[1], feed_recv.at[1], device(1)))
         loads[4].wait()
         both = jnp.concatenate([target[...], target[...]], axis=0)
         lane_half = lax.broadcasted_iota(jnp.int32, both.shape, 0) // 64
         both = jnp.where(lane_half == xl, both, jnp.zeros_like(both))
         tpad[...] = both.T
         tsend[...] = tpad[pl.ds(row0_other, 192), :]
-        pl.semaphore_wait(barrier, len(peers))
-
-        for way in range(2):
-            start(remote(gsend, gbuf.at[0, y], first_send.at[way], ring_recv.at[0, way, 0],
-                         device(1, yy=(y + (7 if way else 1)) % RING)))
-        for i, hi in enumerate((1 - xh, xh)):
-            start(remote(bsend_zero, bbuf.at[0, 0, z, pl.ds(pl.multiple_of(xl * 64, 64), 64)], first_send.at[2 + i],
-                         piece_recv.at[0, 0, xl], device(1, hi=hi, lo=xh)))
-        start(remote(gsend, gbuf.at[0, y], feed_send.at[0], feed_recv.at[0], device(1)))
-        start(remote(cross_state.at[0], cross_fit.at[0], feed_send.at[1], feed_recv.at[1], device(1)))
         swap = remote(tsend, trecv, swap_send, swap_recv, device(0, lo=1 - xl))
         start(swap)
         for d in range(1, RING):
-            to = (z + d) % RING
-            start(remote(expr.at[pl.ds(rows_h, 96), expr_cols(to)], rbuf.at[y, at96(z)],
-                         spread_send.at[d - 1], spread_recv.at[d - 1], device(0, zz=to)))
-        for copy in local:
-            copy.wait()
+            source = (z + RING - d) % RING
+            remote(stage.at[d], rbuf.at[y, at96(source)],
+                   spread_send.at[d - 1], spread_recv.at[d - 1], device(0, zz=source)).wait_recv()
         for part in range(2):
-            ring_start(COLS, part)
+            ring_start(ROWS, part)
         swap.wait_recv()
         for h in range(2):
             tbuf[z, h] = (
                 tpad[pl.ds(pl.multiple_of(row0 + h * 96, 16), 96), :] + trecv[h * 96:(h + 1) * 96, :])
         ring_start(TARGETS, 0)
-        for d in range(1, RING):
-            source = (z + RING - d) % RING
-            remote(expr.at[pl.ds(rows_h, 96), expr_cols(z)], rbuf.at[y, at96(source)],
-                   spread_send.at[d - 1], spread_recv.at[d - 1], device(0, zz=source)).wait_recv()
-        for part in range(2):
-            ring_start(ROWS, part)
 
         loads[5].wait()
         first_lane = xh * 384 + xl * 192
@@ -433,9 +440,13 @@
 
         far = (x + 2) % 4
         make_crosses(1 - xh)
-        grams = grams_of(far)
-        for r in (1, 0):
-            xsend[r, 0, 0:256, :] = grams[r].astype(BF16)
+        for r in (1, 0):
+            gram = jnp.zeros((256, 256), F32)
+            for h in range(2):
+                rows = lhs[r, h, pl.ds(pl.multiple_of((1 - xh) * 256, 256), 256), :]
+                cols = cbuf[h, :, :, pl.ds(pl.multiple_of(xl * 256, 256), 256)].reshape(768, 256)
+                gram += jnp.dot(rows, cols, preferred_element_type=F32)
+            xsend[r, 0, 0:256, :] = gram.astype(BF16)
             xsend[r, 0, 256:320, :] = crosses_of(r, far).astype(BF16)
             start(far_copy(r, 0))
             start(far_copy(r, 1))
@@ -515,6 +526,7 @@
             pltpu.VMEM((2, 2, 128, 256), F32),
             pltpu.VMEM((2, 2, 64, 256), F32),
             pltpu.VMEM((64, 256), BF16),
+            pltpu.VMEM((RING, 96, 128), BF16),
             pltpu.VMEM((2, RING, 96, 512), BF16),
             pltpu.VMEM((RING, 2, 96, 128), BF16),
             pltpu.VMEM((RING, 768, 128), BF16),
@@ -544,6 +556,7 @@
             dma, dma,
             dma((3,)),
             dma((6,)),
+            dma((RING,)),
             dma((4,)),
             dma((2, 7)), dma((2, 7)),
         ],

time: 59.3 us -> 59.3 us (level)
  no operation moved by 1% of the time
where the time goes in v4:
time: 59.3 us; the launch traced here: 59.1 us
  Pallas kernels  58.5 us (99%)
  between operations  0.64 us (1%)
    pallas_call x1, Pallas kernels, body(): pl.pallas_call(kernel, out_shape=out_shape, in_specs=[hbm] * 7, out_specs...  56.7 us
    pallas_call x1, Pallas kernels, body(): pl.pallas_call(copy_out, out_shape=out_shape, in_specs=[hbm] * 3, out_spe...  1.74 us

profile of v4, /device:TPU:1, one launch (start us, length us, event | category | flops | bytes accessed | tf_op | source)
XLA Modules:
  0.0 59.1 jit_solution(13774683533484352661)
XLA Ops:
  0.6 56.7 %shard_map.94 = (f32[256,256]{1,0:T(8,128)}, f32[64,256]{1,0:T(8,128)}, f32[64,256]{1,0:T(8,128)}) custom-call(bf16[384,4096]{1,0:T(8,128)(2,1)} %expr.1, bf16[64,384]{1,0:T(8,128)(2,1)} %bitcast.14, s32[2,6144]{1,0:T(2,128)} %subsample_hbm.1, f32[2,256,256]{2,1,0:T(8,128)} %bitcast.12, f32[2,64,256]{2,1,0:T(8,128)} %bitcast.13, f32[2]{0:T(128)} %step_hbm.1, ...), custom_call_target="tpu_custom_call" | custom-call | tf_op jit(solution)/shard_map/pallas_call | solution.py:510
  57.4 1.7 %shard_map.95 = (f32[256,256]{1,0:T(8,128)}, f32[64,256]{1,0:T(8,128)}, f32[64,256]{1,0:T(8,128)}) custom-call(f32[256,256]{1,0:T(8,128)} %get-tuple-element.9.gram, f32[64,256]{1,0:T(8,128)} %get-tuple-element.10.cross, f32[64,256]{1,0:T(8,128)} %get-tuple-element.11.coef), custom_call_target="tpu_custom_call" | custom-call | tf_op jit(solution)/shard_map/pallas_call | solution.py:574

commit v5 on v4

--- a/solution.py
+++ b/solution.py
@@ -21,7 +21,7 @@
     target, subsample, gram_state, cross_state, step_size, penalty,
     gbuf, bbuf, cross_fit, bsend, acc, precv,
     bsend_zero, stage, cbuf, tbuf, rbuf, lhs, tpad, tsend, trecv, crosses, wbuf, gsend,
-    xsend, xpass, own_block, xrecv, end_part, end_beta, beta_keep,
+    blocks, xsend, xpass, own_block, xrecv, end_part, end_beta, beta_keep,
     ring_send, ring_recv, spread_send, spread_recv, piece_send, piece_recv,
     part_send, part_recv, far_send, far_recv, near_send, near_recv,
     feed_send, feed_recv, end_send, end_recv, own_send, own_recv,
@@ -58,7 +58,7 @@
         copy.start()
         return copy
 
-    def rings(core, view_of, along_y, sent):
+    def rings(core, view_of, along_y):
         def ring_copy(ring, part, way, hop, chunk):
             here = y if ring in along_y else z
             there = (here + (1 if way == 0 else RING - 1)) % RING
@@ -70,23 +70,37 @@
         def ring_start(ring, part):
             here = y if ring in along_y else z
             for way in range(2):
-                copy = ring_copy(ring, part, way, 1, here)
-                copy.start()
-                sent.append(copy)
+                ring_copy(ring, part, way, 1, here).start()
+
+        def arrived(ring, way, hop):
+            here = y if ring in along_y else z
+            return (here + (RING - hop if way == 0 else hop)) % RING
 
         def ring_step(ring, part, hop):
-            here = y if ring in along_y else z
             for way in range(2):
-                if hop == 4 and way != part:
-                    continue
-                chunk = (here + (RING - hop if way == 0 else hop)) % RING
+                chunk = arrived(ring, way, hop)
                 ring_copy(ring, part, way, hop, chunk).wait_recv()
-                if hop < 3 or (hop == 3 and way == part):
-                    copy = ring_copy(ring, part, way, hop + 1, chunk)
-                    copy.start()
-                    sent.append(copy)
-
-        return ring_start, ring_step
+                if way == part:
+                    ring_copy(ring, part, way, hop + 1, chunk).start()
+                else:
+                    @pl.when(hop < 3)
+                    def _():
+                        ring_copy(ring, part, way, hop + 1, chunk).start()
+
+        def ring_last(ring, part):
+            ring_copy(ring, part, part, 4, arrived(ring, part, 4)).wait_recv()
+
+        def ring_drain(ring, part, first=1):
+            @pl.loop(first, 5)
+            def _(hop):
+                for way in range(2):
+                    copy = ring_copy(ring, part, way, hop, arrived(ring, way, hop - 1))
+                    if way == part:
+                        copy.wait_send()
+                    else:
+                        pl.when(hop < 4)(copy.wait_send)
+
+        return ring_start, ring_step, ring_last, ring_drain
 
     def finish_sums():
         for way in range(2):
@@ -121,7 +135,7 @@
                 return gbuf.at[part, chunk]
             return bbuf.at[ring - BETA, part, chunk]
 
-        ring_start, ring_step = rings(1, view_of, (GRAM,), sent)
+        ring_start, ring_step, ring_last, ring_drain = rings(1, view_of, (GRAM,))
         own_k = xl == xh
 
         def own_half(ref_index):
@@ -152,13 +166,22 @@
                 pltpu.make_async_copy(
                     bsend.at[it, r], piece_slot(it, r, lo), piece_recv.at[it, r, lo]).wait()
 
-        def add_products(it, r, distances, first=False):
-            total = None
+        def product_of(it, r, distance):
+            k = ((y if it == 0 else z) + distance) % RING
+            return lax.dot_general(bbuf[it, r, k], gbuf[r, k], ROWS_T, preferred_element_type=F32)
+
+        def first_products(it, r, start_at, count):
+            acc[it, r] = jnp.zeros((128, 256), F32)
+
+            @pl.loop(0, count)
+            def _(j):
+                acc[it, r] += product_of(it, r, start_at + j)
+
+        def add_products(it, r, distances):
+            total = acc[it, r]
             for distance in distances:
-                k = (y + distance) % RING if it == 0 else (z + distance) % RING
-                term = lax.dot_general(bbuf[it, r, k], gbuf[r, k], ROWS_T, preferred_element_type=F32)
-                total = term if total is None else total + term
-            acc[it, r] = total if first else acc[it, r] + total
+                total = total + product_of(it, r, distance)
+            acc[it, r] = total
 
         def part_copy(it, r):
             return remote(acc.at[it, r, own_half(1 - xl)], precv.at[it, r],
@@ -187,28 +210,26 @@
         cross_feed = remote(cross_state.at[0], cross_fit.at[0], feed_send.at[1], feed_recv.at[1], device(0))
         gram_feed = remote(gsend, gbuf.at[0, y], feed_send.at[0], feed_recv.at[0], device(0))
         for r in (1, 0):
-            ring_step(GRAM, r, 1)
             pieces_wait(0, r)
             ring_start(BETA, r)
-        for r in (1, 0):
-            ring_step(BETA, r, 1)
-        for r in (1, 0):
-            ring_step(GRAM, r, 2)
-        for r in (1, 0):
-            ring_step(BETA, r, 2)
-        for r in (1, 0):
-            ring_step(GRAM, r, 3)
-        for hop in (3, 4):
+
+        @pl.loop(1, 4)
+        def _(hop):
+            for r in (1, 0):
+                ring_step(GRAM, r, hop)
             for r in (1, 0):
                 ring_step(BETA, r, hop)
+
+        for r in (1, 0):
+            ring_last(BETA, r)
         cross_feed.wait_recv()
         step, threshold = step_of(0)
         beta_zero = soften(step * cross_fit[0], threshold)
         gram_feed.wait_recv()
         for r in (1, 0):
-            add_products(0, r, (0, 1, 2, 3, 5, 6, 7), first=True)
-        for r in (1, 0):
-            ring_step(GRAM, r, 4)
+            first_products(0, r, 5, 7)
+        for r in (1, 0):
+            ring_last(GRAM, r)
             add_products(0, r, (4,))
             start(part_copy(0, r))
         betas = [beta_zero, beta_one]
@@ -231,8 +252,6 @@
             start(reach_copy(r, M1, z, 1))
             start(reach_copy(r, P1, z, 7))
         for r in (1, 0):
-            add_products(1, r, (0,), first=True)
-        for r in (1, 0):
             reach_copy(r, M2, z + 6, 2).wait_recv()
             start(reach_copy(r, M3, z + 6, 1))
             if r == 0:
@@ -244,7 +263,7 @@
         for r in (1, 0):
             reach_copy(r, M1, z + 7, 1).wait_recv()
             reach_copy(r, P1, z + 1, 7).wait_recv()
-            add_products(1, r, (1, 2, 6, 7))
+            first_products(1, r, 6, 5)
 
         def last_products(r):
             reach_copy(r, M3, z + 5, 1).wait_recv()
@@ -264,6 +283,10 @@
 
         for copy in sent:
             copy.wait_send()
+        ring_drain(GRAM, 1)
+        ring_drain(GRAM, 0, 2)
+        for r in range(2):
+            ring_drain(BETA, r)
         for it, r in ((0, 1), (1, 0), (1, 1)):
             @pl.when(jnp.logical_not(own_k))
             def _():
@@ -292,12 +315,18 @@
             load(0, step_hbm, step_size), load(1, penalty_hbm, penalty), load(2, cross_hbm, cross_state),
             load(3, gram_hbm, gram_state),
         ]
-        stages = [
-            pltpu.make_async_copy(expr.at[pl.ds(rows_h, 96), expr_cols((z + d) % RING)], stage.at[d], stage_sem.at[d])
-            for d in range(1, RING)
-        ]
-        for copy in stages:
-            copy.start()
+        def stage_copy(d):
+            return pltpu.make_async_copy(
+                expr.at[pl.ds(rows_h, 96), expr_cols((z + d) % RING)], stage.at[d], stage_sem.at[d])
+
+        def spread_copy(d, to, source):
+            return remote(stage.at[d], rbuf.at[y, at96(source)], spread_send.at[d - 1], spread_recv.at[d - 1],
+                          device(0, zz=to))
+
+        @pl.loop(1, RING)
+        def _(d):
+            stage_copy(d).start()
+
         local = [
             pltpu.make_async_copy(
                 expr.at[pl.ds(pl.multiple_of(row0 + h * 96, 16), 96), pl.ds(pl.multiple_of(y * 512, 512), 512)],
@@ -322,7 +351,7 @@
                 return tbuf.at[chunk]
             return rbuf.at[chunk, pl.ds(part * 384, 384)]
 
-        ring_start, ring_step = rings(0, view_of, (ROWS,), sent)
+        ring_start, ring_step, ring_last, ring_drain = rings(0, view_of, (ROWS,))
 
         for copy in loads[:4]:
             copy.wait()
@@ -338,10 +367,11 @@
         for i, hi in enumerate((1 - xh, xh)):
             start(remote(bsend_zero, bbuf.at[0, 0, z, pl.ds(pl.multiple_of(xl * 64, 64), 64)], first_send.at[2 + i],
                          piece_recv.at[0, 0, xl], device(1, hi=hi, lo=xh)))
-        for d in range(1, RING):
-            stages[d - 1].wait()
-            start(remote(stage.at[d], rbuf.at[y, at96(z)], spread_send.at[d - 1], spread_recv.at[d - 1],
-                         device(0, zz=(z + d) % RING)))
+        @pl.loop(1, RING)
+        def _(d):
+            stage_copy(d).wait()
+            spread_copy(d, (z + d) % RING, z).start()
+
         for copy in local:
             copy.wait()
         for part in range(2):
@@ -356,10 +386,10 @@
         tsend[...] = tpad[pl.ds(row0_other, 192), :]
         swap = remote(tsend, trecv, swap_send, swap_recv, device(0, lo=1 - xl))
         start(swap)
-        for d in range(1, RING):
-            source = (z + RING - d) % RING
-            remote(stage.at[d], rbuf.at[y, at96(source)],
-                   spread_send.at[d - 1], spread_recv.at[d - 1], device(0, zz=source)).wait_recv()
+        @pl.loop(1, RING)
+        def _(d):
+            spread_copy(d, z, (z + RING - d) % RING).wait_recv()
+
         for part in range(2):
             ring_start(ROWS, part)
         swap.wait_recv()
@@ -388,92 +418,104 @@
             for r in range(2):
                 lhs[r, h, rows, :] = block * pair[r:r + 1, :]
 
-        weigh(0)
-        for hop in (1, 2, 3):
+        @pl.loop(1, 4)
+        def _(hop):
             for part in range(2):
                 ring_step(ROWS, part, hop)
             for part in range(2):
                 ring_step(COLS, part, hop)
             ring_step(TARGETS, 0, hop)
-            weigh(hop)
-            weigh(RING - hop)
+
+            @pl.loop(0, 2)
+            def _(way):
+                weigh((hop - 1) * (1 + 6 * way) % RING)
+
         for part in range(2):
-            ring_step(COLS, part, 4)
-        ring_step(TARGETS, 0, 4)
+            ring_last(COLS, part)
+        ring_last(TARGETS, 0)
+
+        @pl.loop(0, 2)
+        def _(way):
+            weigh(3 + 2 * way)
+
         for part in range(2):
-            ring_step(ROWS, part, 4)
+            ring_last(ROWS, part)
         weigh(4)
 
         def rows_of(hi, h):
             half = pl.ds(pl.multiple_of(hi * 256, 256), 256)
             return jnp.concatenate([lhs[0, h, half, :], lhs[1, h, half, :]], axis=0)
 
-        def grams_of(index):
+        @pl.loop(0, 2)
+        def _(hi):
+            total = jnp.zeros((512, 128), F32)
+            for h in range(2):
+                total += jnp.dot(rows_of(hi, h), tbuf[:, h].reshape(768, 128), preferred_element_type=F32)
+            for r in range(2):
+                crosses[hi, r] = total[r * 256:(r + 1) * 256].T
+
+        def crosses_of(r, index):
+            return crosses[index // 2, r, pl.ds(pl.multiple_of((index % 2) * 64, 64), 64), :]
+
+        top, low = pl.ds(0, 160), pl.ds(160, 160)
+
+        def far_copy(r, half):
+            rows = low if half else top
+            return remote(xsend.at[r, 0, rows], xpass.at[r, rows], far_send.at[r, half], far_recv.at[r, half],
+                          chip_x(left if half else right, 0))
+
+        def near_copy(r, way, half):
+            rows = low if half else top
+            return remote(xsend.at[r, 1 + way, rows], xrecv.at[way, rows], near_send.at[r, way, half],
+                          near_recv.at[way, half], chip_x(left if way else right, r))
+
+        far = (x + 2) % 4
+
+        @pl.loop(0, 4)
+        def _(k):
+            index = (x + 2 + 3 * k + 3 * (k // 2) + 2 * (k // 3)) % 4
             hi, lo = index // 2, index % 2
             total = jnp.zeros((512, 256), F32)
             for h in range(2):
                 cols = cbuf[h, :, :, pl.ds(pl.multiple_of(lo * 256, 256), 256)].reshape(768, 256)
                 total += jnp.dot(rows_of(hi, h), cols, preferred_element_type=F32)
-            return total[0:256], total[256:512]
-
-        def make_crosses(hi):
-            total = jnp.zeros((512, 128), F32)
-            for h in range(2):
-                total += jnp.dot(rows_of(hi, h), tbuf[:, h].reshape(768, 128), preferred_element_type=F32)
-            for r in range(2):
-                crosses[hi, r] = total[r * 256:(r + 1) * 256].T
-
-        def crosses_of(r, index):
-            return crosses[index // 2, r, pl.ds(pl.multiple_of((index % 2) * 64, 64), 64), :]
-
-        top, low = pl.ds(0, 160), pl.ds(160, 160)
-
-        def far_copy(r, half):
-            rows = low if half else top
-            return remote(xsend.at[r, 0, rows], xpass.at[r, rows], far_send.at[r, half], far_recv.at[r, half],
-                          chip_x(left if half else right, 0))
-
-        def near_copy(r, way, half):
-            rows = low if half else top
-            return remote(xsend.at[r, 1 + way, rows], xrecv.at[way, rows], near_send.at[r, way, half],
-                          near_recv.at[way, half], chip_x(left if way else right, r))
-
-        far = (x + 2) % 4
-        make_crosses(1 - xh)
-        for r in (1, 0):
-            gram = jnp.zeros((256, 256), F32)
-            for h in range(2):
-                rows = lhs[r, h, pl.ds(pl.multiple_of((1 - xh) * 256, 256), 256), :]
-                cols = cbuf[h, :, :, pl.ds(pl.multiple_of(xl * 256, 256), 256)].reshape(768, 256)
-                gram += jnp.dot(rows, cols, preferred_element_type=F32)
-            xsend[r, 0, 0:256, :] = gram.astype(BF16)
-            xsend[r, 0, 256:320, :] = crosses_of(r, far).astype(BF16)
-            start(far_copy(r, 0))
-            start(far_copy(r, 1))
-        make_crosses(xh)
-        grams_right = grams_of(right)
-        for r in (1, 0):
-            xsend[r, 1, 160:256, :] = grams_right[r][160:256].astype(BF16)
-            xsend[r, 1, 256:320, :] = crosses_of(r, right).astype(BF16)
-            start(near_copy(r, 0, 1))
-        grams_left = grams_of(left)
-        for r in (1, 0):
-            xsend[r, 2, 0:160, :] = grams_left[r][0:160].astype(BF16)
-            start(near_copy(r, 1, 0))
+            blocks[k] = total
+
+            @pl.when(k == 0)
+            def _():
+                for r in (1, 0):
+                    xsend[r, 0, 0:256, :] = blocks[0, r * 256:(r + 1) * 256].astype(BF16)
+                    xsend[r, 0, 256:320, :] = crosses_of(r, far).astype(BF16)
+                    far_copy(r, 0).start()
+                    far_copy(r, 1).start()
+
+            @pl.when(k == 1)
+            def _():
+                for r in (1, 0):
+                    xsend[r, 1, 160:256, :] = blocks[1, r * 256 + 160:(r + 1) * 256].astype(BF16)
+                    xsend[r, 1, 256:320, :] = crosses_of(r, right).astype(BF16)
+                    near_copy(r, 0, 1).start()
+
+            @pl.when(k == 2)
+            def _():
+                for r in (1, 0):
+                    xsend[r, 2, 0:160, :] = blocks[2, r * 256:r * 256 + 160].astype(BF16)
+                    near_copy(r, 1, 0).start()
+
         for r in (1, 0):
             far_copy(r, 0).wait_recv()
-            xsend[r, 1, 0:160, :] = (grams_right[r][0:160] + xpass[r, 0:160, :].astype(F32)).astype(BF16)
-            start(near_copy(r, 0, 0))
+            xsend[r, 1, 0:160, :] = (
+                blocks[1, r * 256:r * 256 + 160] + xpass[r, 0:160, :].astype(F32)).astype(BF16)
+            near_copy(r, 0, 0).start()
             far_copy(r, 1).wait_recv()
-            xsend[r, 2, 160:256, :] = (grams_left[r][160:256] + xpass[r, 160:256, :].astype(F32)).astype(BF16)
+            xsend[r, 2, 160:256, :] = (
+                blocks[2, r * 256 + 160:(r + 1) * 256] + xpass[r, 160:256, :].astype(F32)).astype(BF16)
             xsend[r, 2, 256:320, :] = (crosses_of(r, left) + xpass[r, 256:320, :].astype(F32)).astype(BF16)
-            start(near_copy(r, 1, 1))
-        grams = grams_of(x)
-        own_block[1, 0:256, :] = grams[1]
-        own_block[1, 256:320, :] = crosses_of(1, x)
+            near_copy(r, 1, 1).start()
+        for r in (1, 0):
+            own_block[r, 0:256, :] = blocks[3, r * 256:(r + 1) * 256]
+            own_block[r, 256:320, :] = crosses_of(r, x)
         start(remote(own_block.at[1], own_block.at[0], own_send, own_recv, device(1)))
-        own_block[0, 0:256, :] = grams[0]
-        own_block[0, 256:320, :] = crosses_of(0, x)
 
         finish_sums()
         for i in range(3):
@@ -483,6 +525,20 @@
         coef_out[...] = soften(end_beta[...] - step * (product - cross_state[0]), threshold)
         for copy in sent:
             copy.wait_send()
+        for part in range(2):
+            ring_drain(COLS, part)
+            ring_drain(ROWS, part)
+        ring_drain(TARGETS, 0)
+
+        @pl.loop(1, RING)
+        def _(d):
+            spread_copy(d, (z + d) % RING, z).wait_send()
+
+        for r in range(2):
+            for half in range(2):
+                far_copy(r, half).wait_send()
+                for way in range(2):
+                    near_copy(r, way, half).wait_send()
 
 
 def copy_out(gram, cross, coef, gram_out, cross_out, coef_out, gram_here, cross_here, coef_here, sems_in, sems_out):
@@ -537,6 +593,7 @@
             pltpu.VMEM((2, 2, 128, 256), F32),
             pltpu.VMEM((2, 2, 768), F32),
             pltpu.VMEM((256, 256), BF16),
+            pltpu.VMEM((4, 512, 256), F32),
             pltpu.VMEM((2, 3, 320, 256), BF16),
             pltpu.VMEM((2, 320, 256), BF16),
             pltpu.VMEM((2, 320, 256), F32),

time: 59.3 us -> 58.7 us (0.990)
  Pallas kernels: 58.5 us -> 57.9 us
where the time goes in v5:
time: 58.7 us; the launch traced here: 58.6 us
  Pallas kernels  57.9 us (99%)
  between operations  0.64 us (1%)
    pallas_call x1, Pallas kernels, body(): pl.pallas_call(kernel, out_shape=out_shape, in_specs=[hbm] * 7, out_specs...  56.2 us
    pallas_call x1, Pallas kernels, body(): pl.pallas_call(copy_out, out_shape=out_shape, in_specs=[hbm] * 3, out_spe...  1.74 us

profile of v5, /device:TPU:1, one launch (start us, length us, event | category | flops | bytes accessed | tf_op | source)
XLA Modules:
  0.0 58.6 jit_solution(15094688738468002480)
XLA Ops:
  0.6 56.2 %shard_map.94 = (f32[256,256]{1,0:T(8,128)}, f32[64,256]{1,0:T(8,128)}, f32[64,256]{1,0:T(8,128)}) custom-call(bf16[384,4096]{1,0:T(8,128)(2,1)} %expr.1, bf16[64,384]{1,0:T(8,128)(2,1)} %bitcast.14, s32[2,6144]{1,0:T(2,128)} %subsample_hbm.1, f32[2,256,256]{2,1,0:T(8,128)} %bitcast.12, f32[2,64,256]{2,1,0:T(8,128)} %bitcast.13, f32[2]{0:T(128)} %step_hbm.1, ...), custom_call_target="tpu_custom_call" | custom-call | tf_op jit(solution)/shard_map/pallas_call | solution.py:566
  56.8 1.7 %shard_map.95 = (f32[256,256]{1,0:T(8,128)}, f32[64,256]{1,0:T(8,128)}, f32[64,256]{1,0:T(8,128)}) custom-call(f32[256,256]{1,0:T(8,128)} %get-tuple-element.9.gram, f32[64,256]{1,0:T(8,128)} %get-tuple-element.10.cross, f32[64,256]{1,0:T(8,128)} %get-tuple-element.11.coef), custom_call_target="tpu_custom_call" | custom-call | tf_op jit(solution)/shard_map/pallas_call | solution.py:631

commit v6 on v5

--- a/solution.py
+++ b/solution.py
@@ -209,14 +209,17 @@
         pieces_start(0, 1)
         cross_feed = remote(cross_state.at[0], cross_fit.at[0], feed_send.at[1], feed_recv.at[1], device(0))
         gram_feed = remote(gsend, gbuf.at[0, y], feed_send.at[0], feed_recv.at[0], device(0))
-        for r in (1, 0):
-            pieces_wait(0, r)
-            ring_start(BETA, r)
-
         @pl.loop(1, 4)
         def _(hop):
             for r in (1, 0):
                 ring_step(GRAM, r, hop)
+
+            @pl.when(hop == 1)
+            def _():
+                for r in (1, 0):
+                    pieces_wait(0, r)
+                    ring_start(BETA, r)
+
             for r in (1, 0):
                 ring_step(BETA, r, hop)
 

time: 58.7 us -> 59.5 us (1.014)
  no operation moved by 1% of the time
where the time goes in v6:
time: 59.5 us; the launch traced here: 58.9 us
  Pallas kernels  58.3 us (98%)
  between operations  0.64 us (1%)
    pallas_call x1, Pallas kernels, body(): pl.pallas_call(kernel, out_shape=out_shape, in_specs=[hbm] * 7, out_specs...  56.6 us
    pallas_call x1, Pallas kernels, body(): pl.pallas_call(copy_out, out_shape=out_shape, in_specs=[hbm] * 3, out_spe...  1.74 us

profile of v6, /device:TPU:1, one launch (start us, length us, event | category | flops | bytes accessed | tf_op | source)
XLA Modules:
  0.0 58.9 jit_solution(15352999356414780404)
XLA Ops:
  0.6 56.6 %shard_map.94 = (f32[256,256]{1,0:T(8,128)}, f32[64,256]{1,0:T(8,128)}, f32[64,256]{1,0:T(8,128)}) custom-call(bf16[384,4096]{1,0:T(8,128)(2,1)} %expr.1, bf16[64,384]{1,0:T(8,128)(2,1)} %bitcast.14, s32[2,6144]{1,0:T(2,128)} %subsample_hbm.1, f32[2,256,256]{2,1,0:T(8,128)} %bitcast.12, f32[2,64,256]{2,1,0:T(8,128)} %bitcast.13, f32[2]{0:T(128)} %step_hbm.1, ...), custom_call_target="tpu_custom_call" | custom-call | tf_op jit(solution)/shard_map/pallas_call | solution.py:569
  57.2 1.7 %shard_map.95 = (f32[256,256]{1,0:T(8,128)}, f32[64,256]{1,0:T(8,128)}, f32[64,256]{1,0:T(8,128)}) custom-call(f32[256,256]{1,0:T(8,128)} %get-tuple-element.9.gram, f32[64,256]{1,0:T(8,128)} %get-tuple-element.10.cross, f32[64,256]{1,0:T(8,128)} %get-tuple-element.11.coef), custom_call_target="tpu_custom_call" | custom-call | tf_op jit(solution)/shard_map/pallas_call | solution.py:634

commit v7 on v5

--- a/solution.py
+++ b/solution.py
@@ -361,21 +361,21 @@
         bsend_zero[...] = soften(step * cross_state[0], threshold).astype(BF16)
         pl.semaphore_wait(barrier, len(peers))
 
+        @pl.loop(1, RING)
+        def _(d):
+            stage_copy(d).wait()
+            spread_copy(d, (z + d) % RING, z).start()
+
+        for copy in local:
+            copy.wait()
+        for part in range(2):
+            ring_start(COLS, part)
         for way in range(2):
             start(remote(gsend, gbuf.at[0, y], first_send.at[way], ring_recv.at[0, way, 0],
                          device(1, yy=(y + (7 if way else 1)) % RING)))
         for i, hi in enumerate((1 - xh, xh)):
             start(remote(bsend_zero, bbuf.at[0, 0, z, pl.ds(pl.multiple_of(xl * 64, 64), 64)], first_send.at[2 + i],
                          piece_recv.at[0, 0, xl], device(1, hi=hi, lo=xh)))
-        @pl.loop(1, RING)
-        def _(d):
-            stage_copy(d).wait()
-            spread_copy(d, (z + d) % RING, z).start()
-
-        for copy in local:
-            copy.wait()
-        for part in range(2):
-            ring_start(COLS, part)
         start(remote(gsend, gbuf.at[0, y], feed_send.at[0], feed_recv.at[0], device(1)))
         start(remote(cross_state.at[0], cross_fit.at[0], feed_send.at[1], feed_recv.at[1], device(1)))
         loads[4].wait()

time: 58.7 us -> 58.7 us (level)
  no operation moved by 1% of the time
where the time goes in v7:
time: 58.7 us; the launch traced here: 58.5 us
  Pallas kernels  57.9 us (99%)
  between operations  0.64 us (1%)
    pallas_call x1, Pallas kernels, body(): pl.pallas_call(kernel, out_shape=out_shape, in_specs=[hbm] * 7, out_specs...  56.1 us
    pallas_call x1, Pallas kernels, body(): pl.pallas_call(copy_out, out_shape=out_shape, in_specs=[hbm] * 3, out_spe...  1.74 us

profile of v7, /device:TPU:1, one launch (start us, length us, event | category | flops | bytes accessed | tf_op | source)
XLA Modules:
  0.0 58.5 jit_solution(18353119066407236103)
XLA Ops:
  0.6 56.1 %shard_map.94 = (f32[256,256]{1,0:T(8,128)}, f32[64,256]{1,0:T(8,128)}, f32[64,256]{1,0:T(8,128)}) custom-call(bf16[384,4096]{1,0:T(8,128)(2,1)} %expr.1, bf16[64,384]{1,0:T(8,128)(2,1)} %bitcast.14, s32[2,6144]{1,0:T(2,128)} %subsample_hbm.1, f32[2,256,256]{2,1,0:T(8,128)} %bitcast.12, f32[2,64,256]{2,1,0:T(8,128)} %bitcast.13, f32[2]{0:T(128)} %step_hbm.1, ...), custom_call_target="tpu_custom_call" | custom-call | tf_op jit(solution)/shard_map/pallas_call | solution.py:566
  56.8 1.7 %shard_map.95 = (f32[256,256]{1,0:T(8,128)}, f32[64,256]{1,0:T(8,128)}, f32[64,256]{1,0:T(8,128)}) custom-call(f32[256,256]{1,0:T(8,128)} %get-tuple-element.9.gram, f32[64,256]{1,0:T(8,128)} %get-tuple-element.10.cross, f32[64,256]{1,0:T(8,128)} %get-tuple-element.11.coef), custom_call_target="tpu_custom_call" | custom-call | tf_op jit(solution)/shard_map/pallas_call | solution.py:631
